TPU v7x, 32 devices: a whole 2x2x4 slice. The times are simulated.
32 devices in a mesh: rows: 16 (over z, x, core), chan: 2 (over y).
Axes of the slice: x: 2, y: 2, z: 4, core: 2. Of those that a mesh axis runs over, the one named last changes fastest.
Arguments:
- hidden: float32 [32, 512, 2048], P('chan', 'rows'), may hold values from -6 to 6
- front: float32 [512, 2048], P('rows', 'chan'), may hold values from -6 to 6
- spectral_weight: float32 [2, 128, 128, 32, 32], P(None, 'rows', 'chan'), may hold values from -0.5 to 0.5
- skip_gain: float32 [32], P('chan'), may hold values from 0.5 to 1.5
- skip_bias: float32 [32], P('chan'), may hold values from -3 to 3
- project_weight: float32 [2, 32], P(None, 'chan'), may hold values from -1 to 1
- project_bias: float32 [2], replicated, may hold values from -3 to 3
- ice_mask: int32 [512, 2048], P('rows', 'chan'), may hold values 0 or 1
- front_flags: int32 [512, 2048], P('rows', 'chan'), may hold values 0 or 1
Outputs:
- velocity: float32 [2, 512, 2048], P(None, 'rows', 'chan')
- front_next: float32 [512, 2048], P('rows', 'chan')
All inputs are finite; a program needn't handle non-finite values. No bound on the sum of `ice_mask` or of `front_flags` on one device may be relied on, other than what follows from the above.
Results may differ from a plain program's by a relative error of at most 0.0003.
Values sent between devices are 32-bit elements; how exact they have to be, the bound alone decides.
A program may use at most 128 MiB of HBM per device.

v0:
```python
import math

import jax
import jax.numpy as jnp
from jax import lax
from jax.sharding import PartitionSpec as P

LS_STEPS = 4


time_step = 0.25
highest = lax.Precision.HIGHEST


def with_halo(block, sides, width):
    for axis, dim in sides:
        count = lax.axis_size(axis)
        forward = [(i, i + 1) for i in range(count - 1)]
        backward = [(target, source) for source, target in forward]
        low = lax.ppermute(
            lax.slice_in_dim(block, block.shape[dim] - width, None, axis=dim), axis, forward
        )
        high = lax.ppermute(lax.slice_in_dim(block, 0, width, axis=dim), axis, backward)
        block = jnp.concatenate([low, block, high], axis=dim)
    return block


def angles(freqs, places, length):
    product = freqs[:, None] * places[None, :] % length
    return 2.0 * math.pi / length * product.astype(jnp.float32)


def x_tables(total_modes, places, length):
    mode_ids = jnp.arange(total_modes, dtype=jnp.int32)
    wave_ids = mode_ids - total_modes * (mode_ids >= total_modes // 2).astype(jnp.int32)
    phase = angles(wave_ids, places, length)
    return jnp.stack([jnp.cos(phase), jnp.sin(phase)])


def forward_x(spectra, tables):
    parts = jnp.einsum("cqrx,spx->cqrsp", spectra, tables, precision=highest)
    real_part = parts[:, :, 0, 0] + parts[:, :, 1, 1]
    imag_part = parts[:, :, 1, 0] - parts[:, :, 0, 1]
    return jnp.stack([real_part, imag_part], axis=2)


def inverse_x(spectra, tables):
    parts = jnp.einsum("cqrp,spx->cqrsx", spectra, tables, precision=highest)
    real_part = parts[:, :, 0, 0] - parts[:, :, 1, 1]
    imag_part = parts[:, :, 0, 1] + parts[:, :, 1, 0]
    stacked = jnp.stack([real_part, imag_part], axis=2)
    return stacked.reshape(stacked.shape[0], stacked.shape[1] * 2, stacked.shape[3])


def advance(padded, speed_x, speed_y, band):
    center = padded[1:-1, 1:-1]
    back_x = center - padded[:-2, 1:-1]
    ahead_x = padded[2:, 1:-1] - center
    back_y = center - padded[1:-1, :-2]
    ahead_y = padded[1:-1, 2:] - center
    transport = jnp.maximum(speed_x, 0.0) * back_x + jnp.minimum(speed_x, 0.0) * ahead_x
    transport = transport + jnp.maximum(speed_y, 0.0) * back_y + jnp.minimum(speed_y, 0.0) * ahead_y
    return center - time_step * band * transport


def on_device(
    hidden,
    front,
    spectral_weight,
    skip_gain,
    skip_bias,
    project_weight,
    project_bias,
    ice_mask,
    front_flags,
):
    local_chan, row_count, columns = hidden.shape
    row_devices = lax.axis_size("rows")
    chan_devices = lax.axis_size("chan")
    local_ymodes = spectral_weight.shape[1]
    all_rows = row_count * row_devices
    all_xmodes = spectral_weight.shape[2] * chan_devices
    all_ymodes = local_ymodes * row_devices
    norm_scale = 1.0 / math.sqrt(all_rows * columns * all_xmodes * all_ymodes)
    y_ids = jnp.arange(all_ymodes, dtype=jnp.int32)
    y_phase = angles(y_ids, jnp.arange(columns, dtype=jnp.int32), columns)
    forward_y = jnp.stack([jnp.cos(y_phase), -jnp.sin(y_phase)], axis=1).reshape(
        2 * all_ymodes, columns
    )
    y_weights = jnp.where(y_ids == 0, 1.0, 2.0).astype(jnp.float32)[:, None] * norm_scale
    inverse_y = jnp.stack(
        [y_weights * jnp.cos(y_phase), -y_weights * jnp.sin(y_phase)], axis=1
    ).reshape(2 * all_ymodes, columns)
    spec_y = jnp.einsum("cxy,ky->ckx", hidden, forward_y, precision=highest)
    own_rows = lax.axis_index("rows") * row_count + jnp.arange(row_count, dtype=jnp.int32)
    local_tables = x_tables(all_xmodes, own_rows, all_rows)
    picked = spec_y
    picked = picked.reshape(local_chan, local_ymodes * lax.axis_size("rows"), 2, row_count)
    owned = lax.psum_scatter(
        jnp.transpose(forward_x(picked, local_tables), (1, 0, 2, 3)),
        "rows",
        scatter_dimension=0,
        tiled=True,
    )
    spectra = jnp.transpose(owned, (1, 0, 2, 3))
    gathered = lax.all_to_all(spectra, "chan", split_axis=3, concat_axis=0, tiled=True)
    real_in = gathered[:, :, 0]
    imag_in = gathered[:, :, 1]
    real_out = jnp.einsum(
        "qpio,iqp->oqp", spectral_weight[0], real_in, precision=highest
    ) - jnp.einsum("qpio,iqp->oqp", spectral_weight[1], imag_in, precision=highest)
    imag_out = jnp.einsum(
        "qpio,iqp->oqp", spectral_weight[0], imag_in, precision=highest
    ) + jnp.einsum("qpio,iqp->oqp", spectral_weight[1], real_in, precision=highest)
    mixed = lax.all_to_all(
        jnp.stack([real_out, imag_out], axis=2), "chan", split_axis=0, concat_axis=3, tiled=True
    )
    inverted = inverse_x(lax.all_gather(mixed, "rows", axis=1, tiled=True), local_tables)
    spectral = jnp.einsum("ckx,ky->cxy", inverted, inverse_y, precision=highest)
    activated = jax.nn.gelu(
        spectral + skip_gain[:, None, None] * hidden + skip_bias[:, None, None], approximate=False
    )
    partial_speed = jnp.einsum("jc,cxy->jxy", project_weight, activated, precision=highest)
    tile_speed = (
        lax.psum_scatter(partial_speed, "chan", scatter_dimension=2, tiled=True)
        + project_bias[:, None, None]
    )
    velocity = tile_speed * ice_mask.astype(jnp.float32)[None]
    band = front_flags.astype(jnp.float32)
    level = front
    for level_step in range(LS_STEPS):
        padded = with_halo(level, (("rows", 0), ("chan", 1)), 1)
        level = advance(padded, velocity[0], velocity[1], band)
    return (velocity, level)


def solution(mesh):
    return jax.shard_map(
        on_device,
        mesh=mesh,
        in_specs=(
            P("chan", "rows", None),
            P("rows", "chan"),
            P(None, "rows", "chan", None, None),
            P("chan"),
            P("chan"),
            P(None, "chan"),
            P(),
            P("rows", "chan"),
            P("rows", "chan"),
        ),
        out_specs=(P(None, "rows", "chan"), P("rows", "chan")),
        check_vma=False,
    )
```

profile of v0, /device:TPU:3, one launch (start us, length us, event | category | flops | bytes accessed | tf_op | source)
XLA Modules:
  0.0 339.4 jit_solution(6177520887231481637)
XLA Ops:
  7.2 4.1 %fusion.38 = (f32[128,1,2048]{2,0,1:T(8,128)S(1)}, f32[128,1,2048]{2,0,1:T(8,128)S(1)}) fusion(), kind=kLoop, calls=%fused_computation.62 | loop fusion | flops 3932160 | bytes 2097152 | tf_op jit(solution)/shard_map/cos | solution.py:87
  11.6 1.6 copy.68
  13.2 2.6 reshape.371
  15.8 6.1 %convolution_bitcast_fusion = f32[16,256,32]{1,2,0:T(8,128)S(1)} fusion(f32[256,2048,1]{1,0,2:T(8,128)} %reshape.371, f32[16,32,2048]{2,1,0:T(8,128)} %param.9), kind=kOutput, calls=%fused_computation.43 | convolution fusion | flops 3221225472 | bytes 6815744 | tf_op jit(solution)/shard_map/cxy,ky->ckx/dot_general | solution.py:94
  22.0 1.3 copy.69
  23.4 4.4 %fusion.23 = f32[16,128,2,2,128]{4,1,3,2,0:T(8,128)S(1)} fusion(f32[16,128,2,32,1]{3,0,2,1,4:T(8,128)S(1)} %bitcast.137, f32[1,128,32]{1,2,0:T(8,128)S(1)} %get-tuple-element.39, f32[1,128,32]{1,2,0:T(8,128)S(1)} %get-tuple-element.38), kind=kOutput, calls=%fused_computation.38 | convolution fusion | flops 402661376 | bytes 4751360 | tf_op jit(solution)/shard_map/cqrx,spx->cqrsp/dot_general | solution.py:41
  28.1 1.5 maximum_bitcast_fusion
  29.7 60.7 %reduce-scatter.5.cloned.1.call-done = f32[8,16,2,128]{3,0,1,2:T(8,128)} async-done(((f32[128,16,2,128]{3,0,1,2:T(8,128)}), f32[8,16,2,128]{3,0,1,2:T(8,128)}) %reduce-scatter.5.cloned.1.call-update) | async-done | bytes 131088 | tf_op jit(solution)/shard_map/reduce_scatter | solution.py:99
  90.3 1.4 copy.73
  92.1 5.7 %all_to_all.36 = f32[2,1,16384]{2,1,0:T(1,128)S(1)} all-to-all(f32[2,1,16384]{2,1,0:T(1,128)S(1)} %reshape.389), channel_id=1, replica_groups=mesh['rows'=16,'chan'=2] {'chan'}, dimensions={0} | all-to-all | bytes 262144 | tf_op jit(solution)/shard_map/all_to_all | solution.py:106
  98.3 1.0 reduce.8
  100.5 4.5 %fusion.5 = (f32[8,64,32]{1,2,0:T(8,128)S(1)}, f32[8,64,32]{1,2,0:T(8,128)S(1)}, f32[8,64,32]{1,2,0:T(8,128)S(1)}, f32[8,64,32]{1,2,0:T(8,128)S(1)}) fusion(f32[2,8,64,32,32]{2,4,3,1,0:T(8,128)} %param.11, f32[8,64,32]{1,2,0:T(8,128)S(1)} %copy.126, f32[8,64,32]{1,2,0:T(8,128)S(1)} %copy.127), kind=kLoop, calls=%fused_computation.11 | loop fusion | flops 4128768 | bytes 4587520
  105.6 5.7 %all_to_all.37 = f32[2,1,16384]{2,1,0:T(1,128)S(1)} all-to-all(f32[2,1,16384]{2,1,0:T(1,128)S(1)} %reshape.391), channel_id=1, replica_groups=mesh['rows'=16,'chan'=2] {'chan'}, dimensions={0} | all-to-all | bytes 262144 | tf_op jit(solution)/shard_map/all_to_all | solution.py:115
  111.3 1.0 reduce.9
  112.7 0.8 all_to_all.33
  114.1 4.2 %broadcast_multiply_fusion = (f32[128,1,2048]{2,0,1:T(8,128)S(1)}, f32[128,1,2048]{2,0,1:T(8,128)S(1)}) fusion(f32[128]{0:T(128)S(1)} %fusion.105, f32[128]{0:T(128)S(1)} %fusion.104), kind=kLoop, calls=%fused_computation.59 | loop fusion | flops 4194304 | bytes 2098176 | tf_op jit(solution)/shard_map/mul | solution.py:92
  118.3 39.6 %all-gather.2.cloned.1.call-done = f32[16,128,2,128]{3,1,2,0:T(8,128)} async-done(((f32[16,8,2,128]{3,1,2,0:T(8,128)}), f32[16,128,2,128]{3,1,2,0:T(8,128)}) %all-gather.2.cloned.1.call-update) | async-done | bytes 2097168 | tf_op jit(solution)/shard_map/all_gather | solution.py:118
  157.9 4.1 %fusion.21 = f32[16,128,2,2,32]{1,4,3,2,0:T(8,128)S(1)} fusion(f32[16,128,2,128]{3,1,2,0:T(8,128)} %all-gather.2.cloned.1.call-done, f32[1,128,32]{1,2,0:T(8,128)S(1)} %get-tuple-element.39, f32[1,128,32]{1,2,0:T(8,128)S(1)} %get-tuple-element.38), kind=kOutput, calls=%fused_computation.36 | convolution fusion | flops 402661376 | bytes 3178496 | tf_op jit(solution)/shard_map/cqrp,spx->cqrsx/dot_general | solution.py:48
  162.1 13.0 %fusion.1 = f32[16,32,2048]{2,1,0:T(8,128)S(1)} fusion(f32[16,32,2048]{2,1,0:T(8,128)S(1)} %copy-done.1, f32[128,1,2048]{2,0,1:T(8,128)S(1)} %get-tuple-element.42, f32[128,1,2048]{2,0,1:T(8,128)S(1)} %get-tuple-element.43, f32[16]{0:T(128)S(1)} %copy-done.7, f32[16]{0:T(128)S(1)} %copy-done.8, f32[16,128,1,32]{1,3,0,2:T(8,128)S(1)} %fusion.40, ...), kind=kOutput, calls=%fused_computation.2 | convolution fusion | flops 3292135424 | bytes 11010176 | tf_op jit(solution)/shard_map/ckx,ky->cxy/dot_general | solution.py:119
  175.1 4.9 %fusion.16 = f32[2,32,2048]{2,0,1:T(2,128)S(1)} fusion(f32[16,32,2048]{2,1,0:T(8,128)S(1)} %fusion.1, f32[2,16]{1,0:T(2,128)S(1)} %copy-done), kind=kOutput, calls=%fused_computation.30 | convolution fusion | flops 25165824 | bytes 4718720 | tf_op jit(solution)/shard_map/jc,cxy->jxy/dot_general | solution.py:123
  180.0 26.2 %copy.119 = f32[2,32,2048]{0,1,2:T(8,128)} copy(f32[2,32,2048]{2,0,1:T(2,128)S(1)} %fusion.16) | data formatting | bytes 1048576
  206.2 28.6 %reshape.387 = f32[2048,64]{1,0:T(8,128)} reshape(f32[2048,32,2]{2,1,0:T(8,128)} %bitcast.135) | data formatting | bytes 1048576
  234.8 2.8 collective-permute-start
  237.7 1.9 collective-permute-start.1
  239.6 3.9 %collective-permute-done.1 = f32[1,1024]{1,0:T(1,128)S(1)} collective-permute-done((f32[1,1024]{1,0:T(1,128)S(1)}, f32[1,1024]{1,0:T(1,128)S(1)}, u32[]{:S(2)}, u32[]{:S(2)}) %collective-permute-start.1) | collective-permute-done | bytes 4128 | tf_op jit(solution)/shard_map/ppermute | solution.py:23
  243.6 3.3 collective-permute-start.2
  246.9 1.3 collective-permute-start.3
  248.2 6.3 %reduce-scatter.7.cloned.1.call-done = f32[1024,64]{1,0:T(8,128)} async-done(((f32[2048,64]{1,0:T(8,128)}), f32[1024,64]{1,0:T(8,128)}) %reduce-scatter.7.cloned.1.call-update) | async-done | bytes 262160
  254.5 19.5 %reshape.388 = f32[1024,32,2]{2,1,0:T(8,128)} reshape(f32[1024,64]{1,0:T(8,128)} %reduce-scatter.7.cloned.1.call-done) | data formatting | bytes 524288
  274.0 10.0 %copy.120 = f32[2,32,1024]{2,0,1:T(2,128)S(1)} copy(f32[2,32,1024]{0,1,2:T(8,128)} %bitcast.136) | data formatting | bytes 524288
  284.8 3.7 %collective-permute-start.4 = (f32[1,1024]{1,0:T(1,128)S(1)}, f32[1,1024]{1,0:T(1,128)S(1)}, u32[]{:S(2)}, u32[]{:S(2)}) collective-permute-start(f32[1,1024]{1,0:T(1,128)S(1)} %get-tuple-element.34), channel_id=1, source_target_pairs={{0,2},{2,4},{4,6},{6,8},{8,10},{10,12},{12,14},{14,16},{16,18},{18... | collective-permute-start | bytes 12296 | tf_op jit(solution)/shard_map/ppermute | solution.py:20
  288.4 1.9 collective-permute-start.5
  290.4 3.9 %collective-permute-done.5 = f32[1,1024]{1,0:T(1,128)S(1)} collective-permute-done((f32[1,1024]{1,0:T(1,128)S(1)}, f32[1,1024]{1,0:T(1,128)S(1)}, u32[]{:S(2)}, u32[]{:S(2)}) %collective-permute-start.5) | collective-permute-done | bytes 4128 | tf_op jit(solution)/shard_map/ppermute | solution.py:23
  294.4 2.2 collective-permute-start.6
  296.5 1.3 collective-permute-start.7
  297.8 3.2 collective-permute-done.7
  301.2 3.4 %collective-permute-start.8 = (f32[1,1024]{1,0:T(1,128)S(1)}, f32[1,1024]{1,0:T(1,128)S(1)}, u32[]{:S(2)}, u32[]{:S(2)}) collective-permute-start(f32[1,1024]{1,0:T(1,128)S(1)} %get-tuple-element.32), channel_id=1, source_target_pairs={{0,2},{2,4},{4,6},{6,8},{8,10},{10,12},{12,14},{14,16},{16,18},{18... | collective-permute-start | bytes 12296 | tf_op jit(solution)/shard_map/ppermute | solution.py:20
  304.6 1.9 collective-permute-start.9
  306.6 3.9 %collective-permute-done.9 = f32[1,1024]{1,0:T(1,128)S(1)} collective-permute-done((f32[1,1024]{1,0:T(1,128)S(1)}, f32[1,1024]{1,0:T(1,128)S(1)}, u32[]{:S(2)}, u32[]{:S(2)}) %collective-permute-start.9) | collective-permute-done | bytes 4128 | tf_op jit(solution)/shard_map/ppermute | solution.py:23
  310.5 1.3 collective-permute-start.10
  311.9 1.3 collective-permute-start.11
  313.2 3.2 collective-permute-done.11
  316.6 3.4 collective-permute-start.12
  320.0 1.9 collective-permute-start.13
  321.9 3.9 %collective-permute-done.13 = f32[1,1024]{1,0:T(1,128)S(1)} collective-permute-done((f32[1,1024]{1,0:T(1,128)S(1)}, f32[1,1024]{1,0:T(1,128)S(1)}, u32[]{:S(2)}, u32[]{:S(2)}) %collective-permute-start.13) | collective-permute-done | bytes 4128 | tf_op jit(solution)/shard_map/ppermute | solution.py:23
  325.9 1.3 collective-permute-start.14
  327.2 1.3 collective-permute-start.15
  328.6 3.2 collective-permute-done.15
  (73 shorter events, 6.5 us)
Async XLA Ops:
  7.2 167.9 %copy-start = (f32[2,16]{1,0:T(2,128)S(1)}, f32[2,16]{1,0:T(2,128)}, u32[]{:S(2)}) copy-start(f32[2,16]{1,0:T(2,128)} %param.14) | copy-start | bytes 388
  7.2 83.2 %reduce-scatter.5.cloned.1.call-start = ((), (), s32[]{:S(2)}) async-start(), calls=%async_computation.4 | async-start | bytes 2228224 | tf_op jit(solution)/shard_map/reduce_scatter | solution.py:99
  29.6 128.2 %all-gather.2.cloned.1.call-start = ((), (), s32[]{:S(2)}) async-start(), calls=%async_computation.5 | async-start | bytes 2228224 | tf_op jit(solution)/shard_map/all_gather | solution.py:118
  112.3 49.8 %copy-start.7 = (f32[16]{0:T(128)S(1)}, f32[16]{0:T(128)}, u32[]{:S(2)}) copy-start(f32[16]{0:T(128)} %param.13) | copy-start | bytes 196
  112.3 49.8 %copy-start.8 = (f32[16]{0:T(128)S(1)}, f32[16]{0:T(128)}, u32[]{:S(2)}) copy-start(f32[16]{0:T(128)} %param.12) | copy-start | bytes 196
  113.6 140.9 %reduce-scatter.7.cloned.1.call-start = ((), (), s32[]{:S(2)}) async-start(), calls=%async_computation.6 | async-start | bytes 1572864
  157.9 4.2 %copy-start.1 = (f32[16,32,2048]{2,1,0:T(8,128)S(1)}, f32[16,32,2048]{2,1,0:T(8,128)}, u32[]{:S(2)}) copy-start(f32[16,32,2048]{2,1,0:T(8,128)} %param.9) | copy-start | bytes 12582916
  206.2 28.6 %copy-start.4 = (f32[32,1024]{1,0:T(8,128)S(1)}, f32[32,1024]{1,0:T(8,128)}, u32[]{:S(2)}) copy-start(f32[32,1024]{1,0:T(8,128)} %param.10) | copy-start | bytes 393220
  206.2 33.4 %copy-start.5 = (s32[32,1024]{1,0:T(8,128)S(1)}, s32[32,1024]{1,0:T(8,128)}, u32[]{:S(2)}) copy-start(s32[32,1024]{1,0:T(8,128)} %param.16) | copy-start | bytes 393220
  234.8 4.8 %collective-permute-start = (f32[1,1024]{1,0:T(1,128)S(1)}, f32[1,1024]{1,0:T(1,128)S(1)}, u32[]{:S(2)}, u32[]{:S(2)}) collective-permute-start(f32[1,1024]{1,0:T(1,128)S(1)} %get-tuple-element.36), channel_id=1, source_target_pairs={{0,2},{2,4},{4,6},{6,8},{8,10},{10,12},{12,14},{14,16},{16,18},{18... | collective-permute-start | bytes 12296 | tf_op jit(solution)/shard_map/ppermute | solution.py:20
  237.7 5.8 %collective-permute-start.1 = (f32[1,1024]{1,0:T(1,128)S(1)}, f32[1,1024]{1,0:T(1,128)S(1)}, u32[]{:S(2)}, u32[]{:S(2)}) collective-permute-start(f32[1,1024]{1,0:T(1,128)S(1)} %get-tuple-element.37), channel_id=1, source_target_pairs={{2,0},{4,2},{6,4},{8,6},{10,8},{12,10},{14,12},{16,14},{18,16},{20... | collective-permute-start | bytes 12296 | tf_op jit(solution)/shard_map/ppermute | solution.py:23
  243.6 41.0 %collective-permute-start.2 = (f32[34,1]{1,0:T(8,128)S(1)}, f32[34,1]{1,0:T(8,128)S(1)}, u32[]{:S(2)}, u32[]{:S(2)}) collective-permute-start(f32[34,1]{1,0:T(8,128)S(1)} %get-tuple-element.28), channel_id=1, source_target_pairs={{0,1},{2,3},{4,5},{6,7},{8,9},{10,11},{12,13},{14,15},{16,17},{18,... | collective-permute-start | bytes 416 | tf_op jit(solution)/shard_map/ppermute | solution.py:20
  246.9 37.7 %collective-permute-start.3 = (f32[34,1]{1,0:T(8,128)S(1)}, f32[34,1]{1,0:T(8,128)S(1)}, u32[]{:S(2)}, u32[]{:S(2)}) collective-permute-start(f32[34,1]{1,0:T(8,128)S(1)} %get-tuple-element.29), channel_id=1, source_target_pairs={{1,0},{3,2},{5,4},{7,6},{9,8},{11,10},{13,12},{15,14},{17,16},{19,... | collective-permute-start | bytes 416 | tf_op jit(solution)/shard_map/ppermute | solution.py:23
  274.0 10.0 %copy-start.6 = (f32[2]{0:T(128)S(1)}, f32[2]{0:T(128)}, u32[]{:S(2)}) copy-start(f32[2]{0:T(128)} %param.15) | copy-start | bytes 28
  274.0 10.6 %copy-start.3 = (s32[32,1024]{1,0:T(8,128)S(1)}, s32[32,1024]{1,0:T(8,128)}, u32[]{:S(2)}) copy-start(s32[32,1024]{1,0:T(8,128)} %param.17) | copy-start | bytes 393220
  284.5 48.1 %copy-start.2 = (f32[2,32,1024]{2,1,0:T(8,128)}, f32[2,32,1024]{2,1,0:T(8,128)S(1)}, u32[]{:S(2)}) copy-start(f32[2,32,1024]{2,1,0:T(8,128)S(1)} %copy.83) | copy-start | bytes 786436
  284.8 5.6 %collective-permute-start.4 = (f32[1,1024]{1,0:T(1,128)S(1)}, f32[1,1024]{1,0:T(1,128)S(1)}, u32[]{:S(2)}, u32[]{:S(2)}) collective-permute-start(f32[1,1024]{1,0:T(1,128)S(1)} %get-tuple-element.34), channel_id=1, source_target_pairs={{0,2},{2,4},{4,6},{6,8},{8,10},{10,12},{12,14},{14,16},{16,18},{18... | collective-permute-start | bytes 12296 | tf_op jit(solution)/shard_map/ppermute | solution.py:20
  288.4 5.8 %collective-permute-start.5 = (f32[1,1024]{1,0:T(1,128)S(1)}, f32[1,1024]{1,0:T(1,128)S(1)}, u32[]{:S(2)}, u32[]{:S(2)}) collective-permute-start(f32[1,1024]{1,0:T(1,128)S(1)} %get-tuple-element.35), channel_id=1, source_target_pairs={{2,0},{4,2},{6,4},{8,6},{10,8},{12,10},{14,12},{16,14},{18,16},{20... | collective-permute-start | bytes 12296 | tf_op jit(solution)/shard_map/ppermute | solution.py:23
  294.4 3.5 %collective-permute-start.6 = (f32[34,1]{1,0:T(8,128)S(1)}, f32[34,1]{1,0:T(8,128)S(1)}, u32[]{:S(2)}, u32[]{:S(2)}) collective-permute-start(f32[34,1]{1,0:T(8,128)S(1)} %get-tuple-element.26), channel_id=1, source_target_pairs={{0,1},{2,3},{4,5},{6,7},{8,9},{10,11},{12,13},{14,15},{16,17},{18,... | collective-permute-start | bytes 416 | tf_op jit(solution)/shard_map/ppermute | solution.py:20
  296.5 4.5 %collective-permute-start.7 = (f32[34,1]{1,0:T(8,128)S(1)}, f32[34,1]{1,0:T(8,128)S(1)}, u32[]{:S(2)}, u32[]{:S(2)}) collective-permute-start(f32[34,1]{1,0:T(8,128)S(1)} %get-tuple-element.27), channel_id=1, source_target_pairs={{1,0},{3,2},{5,4},{7,6},{9,8},{11,10},{13,12},{15,14},{17,16},{19,... | collective-permute-start | bytes 416 | tf_op jit(solution)/shard_map/ppermute | solution.py:23
  301.2 5.3 %collective-permute-start.8 = (f32[1,1024]{1,0:T(1,128)S(1)}, f32[1,1024]{1,0:T(1,128)S(1)}, u32[]{:S(2)}, u32[]{:S(2)}) collective-permute-start(f32[1,1024]{1,0:T(1,128)S(1)} %get-tuple-element.32), channel_id=1, source_target_pairs={{0,2},{2,4},{4,6},{6,8},{8,10},{10,12},{12,14},{14,16},{16,18},{18... | collective-permute-start | bytes 12296 | tf_op jit(solution)/shard_map/ppermute | solution.py:20
  304.6 5.8 %collective-permute-start.9 = (f32[1,1024]{1,0:T(1,128)S(1)}, f32[1,1024]{1,0:T(1,128)S(1)}, u32[]{:S(2)}, u32[]{:S(2)}) collective-permute-start(f32[1,1024]{1,0:T(1,128)S(1)} %get-tuple-element.33), channel_id=1, source_target_pairs={{2,0},{4,2},{6,4},{8,6},{10,8},{12,10},{14,12},{16,14},{18,16},{20... | collective-permute-start | bytes 12296 | tf_op jit(solution)/shard_map/ppermute | solution.py:23
  310.5 2.7 collective-permute-start.10
  311.9 4.5 %collective-permute-start.11 = (f32[34,1]{1,0:T(8,128)S(1)}, f32[34,1]{1,0:T(8,128)S(1)}, u32[]{:S(2)}, u32[]{:S(2)}) collective-permute-start(f32[34,1]{1,0:T(8,128)S(1)} %get-tuple-element.25), channel_id=1, source_target_pairs={{1,0},{3,2},{5,4},{7,6},{9,8},{11,10},{13,12},{15,14},{17,16},{19,... | collective-permute-start | bytes 416 | tf_op jit(solution)/shard_map/ppermute | solution.py:23
  316.6 5.3 %collective-permute-start.12 = (f32[1,1024]{1,0:T(1,128)S(1)}, f32[1,1024]{1,0:T(1,128)S(1)}, u32[]{:S(2)}, u32[]{:S(2)}) collective-permute-start(f32[1,1024]{1,0:T(1,128)S(1)} %get-tuple-element.30), channel_id=1, source_target_pairs={{0,2},{2,4},{4,6},{6,8},{8,10},{10,12},{12,14},{14,16},{16,18},{18... | collective-permute-start | bytes 12296 | tf_op jit(solution)/shard_map/ppermute | solution.py:20
  320.0 5.8 %collective-permute-start.13 = (f32[1,1024]{1,0:T(1,128)S(1)}, f32[1,1024]{1,0:T(1,128)S(1)}, u32[]{:S(2)}, u32[]{:S(2)}) collective-permute-start(f32[1,1024]{1,0:T(1,128)S(1)} %get-tuple-element.31), channel_id=1, source_target_pairs={{2,0},{4,2},{6,4},{8,6},{10,8},{12,10},{14,12},{16,14},{18,16},{20... | collective-permute-start | bytes 12296 | tf_op jit(solution)/shard_map/ppermute | solution.py:23
  325.9 2.7 collective-permute-start.14
  327.2 4.5 %collective-permute-start.15 = (f32[34,1]{1,0:T(8,128)S(1)}, f32[34,1]{1,0:T(8,128)S(1)}, u32[]{:S(2)}, u32[]{:S(2)}) collective-permute-start(f32[34,1]{1,0:T(8,128)S(1)} %get-tuple-element.23), channel_id=1, source_target_pairs={{1,0},{3,2},{5,4},{7,6},{9,8},{11,10},{13,12},{15,14},{17,16},{19,... | collective-permute-start | bytes 416 | tf_op jit(solution)/shard_map/ppermute | solution.py:23
Sparse Core Ops, SparseCore 0:
  29.7 60.5 reduce-scatter.4
  113.7 44.0 all-gather.1
  234.9 19.5 reduce-scatter.6
where the time goes:
time: 345 us; the launch traced here: 339 us
  waiting for transfers between devices  132 us (38%)
  local copies, waits for them, and re-layouts  94.8 us (27%)
  starting transfers between devices  34.8 us (10%)
  matrix products  32.5 us (9%)
  other arithmetic  19.5 us (6%)
  between operations  14.6 us (4%)
  blocking collectives  11.4 us (3%)
    unnamed x30, local copies, waits for them, and re-layouts  85.6 us
    reduce_scatter x1, waiting for transfers between devices, on_device(): lax.psum_scatter(jnp.transpose(forward_x(picked, local_tables), (1, 0, 2,...  60.7 us
    all_gather x1, waiting for transfers between devices, on_device(): lax.all_gather(mixed, 'rows', axis=1, tiled=True)  39.6 us
    ppermute x8, waiting for transfers between devices, with_halo(): lax.ppermute(lax.slice_in_dim(block, 0, width, axis=dim), axis, backward)  25.2 us
    ppermute x8, starting transfers between devices, with_halo(): lax.ppermute(lax.slice_in_dim(block, block.shape[dim] - width, None, axis...  21.4 us
    dot_general x1, matrix products, on_device(): spectral = jnp.einsum('ckx,ky->cxy', inverted, inverse_y, precision=highest)  13 us
    ppermute x8, starting transfers between devices, with_halo(): lax.ppermute(lax.slice_in_dim(block, 0, width, axis=dim), axis, backward)  12.9 us
  transfers between devices with their start and end apart: 19, of which 10 were waited for; matrix products, arithmetic and copies ran while one was open for 10% of the time, Pallas kernels for 0%

commit v1 on v0

v1 whole, which is shorter than its diff:
```python
import math

import jax
import jax.numpy as jnp
import numpy as np
from jax import lax
from jax.sharding import PartitionSpec as P

LS_STEPS = 4
time_step = 0.25
high = lax.Precision.HIGH


def np_angles(freqs, places, length):
    return 2.0 * math.pi / length * ((freqs[:, None] * places[None, :]) % length)


def with_halo(block, axis, dim, width):
    count = lax.axis_size(axis)
    forward = [(i, i + 1) for i in range(count - 1)]
    backward = [(target, source) for source, target in forward]
    size = block.shape[dim]
    low = lax.ppermute(lax.slice_in_dim(block, size - width, None, axis=dim), axis, forward)
    up = lax.ppermute(lax.slice_in_dim(block, 0, width, axis=dim), axis, backward)
    return jnp.concatenate([low, block, up], axis=dim)


def advance(phi, u, v, band):
    center = phi[1:-1, 1:-1]
    back_x = center - phi[:-2, 1:-1]
    ahead_x = phi[2:, 1:-1] - center
    back_y = center - phi[1:-1, :-2]
    ahead_y = phi[1:-1, 2:] - center
    transport = jnp.maximum(u, 0.0) * back_x + jnp.minimum(u, 0.0) * ahead_x
    transport = transport + jnp.maximum(v, 0.0) * back_y + jnp.minimum(v, 0.0) * ahead_y
    return center - time_step * band * transport


def on_device(
    hidden,
    front,
    spectral_weight,
    skip_gain,
    skip_bias,
    project_weight,
    project_bias,
    ice_mask,
    front_flags,
):
    cl, rc, ny = hidden.shape
    R = lax.axis_size("rows")
    D = lax.axis_size("chan")
    ql = spectral_weight.shape[1]
    pl_ = spectral_weight.shape[2]
    nx = rc * R
    mx = pl_ * D
    my = ql * R
    scale = 1.0 / math.sqrt(nx * ny * mx * my)
    yph = np_angles(np.arange(my), np.arange(ny), ny)
    fy = np.stack([np.cos(yph), -np.sin(yph)], axis=1).reshape(2 * my, ny).astype(np.float32)
    w = np.where(np.arange(my) == 0, 1.0, 2.0)[:, None] * scale
    iy = np.stack([w * np.cos(yph), -w * np.sin(yph)], axis=1).reshape(2 * my, ny).astype(np.float32)
    pid = np.arange(mx)
    kp = np.where(pid < mx // 2, pid, pid - mx)
    xph = np_angles(kp, np.arange(nx), nx)
    cx = np.cos(xph).astype(np.float32)
    sx = np.sin(xph).astype(np.float32)
    fx = np.stack([np.stack([cx, -sx]), np.stack([sx, cx])]).transpose(0, 3, 1, 2).reshape(2, nx, 2 * mx)
    ix = np.stack([np.stack([cx, sx]), np.stack([-sx, cx])]).reshape(2, 2, mx, nx)

    spec_y = jnp.einsum("ky,cxy->kcx", jnp.asarray(fy), hidden, precision=high)
    recv = lax.all_to_all(spec_y.reshape(R, ql, 2, cl, rc), "rows", 0, 0, tiled=True)
    spec = jnp.einsum(
        "sqrcx,rsxP->qcP", recv, jnp.asarray(fx).reshape(2, R, rc, 2 * mx), precision=high
    ).reshape(ql, cl, 2, D, pl_)
    spec = lax.all_to_all(spec.transpose(3, 1, 2, 0, 4), "chan", 0, 0, tiled=True)
    spec = spec.reshape(D * cl, 2, ql, pl_)
    wt = spectral_weight.transpose(0, 3, 4, 1, 2)
    a, b = spec[:, 0][:, None], spec[:, 1][:, None]
    re = jnp.sum(wt[0] * a - wt[1] * b, axis=0)
    im = jnp.sum(wt[0] * b + wt[1] * a, axis=0)
    mixed = jnp.stack([re, im], axis=1).reshape(D, cl, 2, ql, pl_)
    mixed = lax.all_to_all(mixed, "chan", 0, 0, tiled=True)
    inv = jnp.einsum(
        "dcrqp,rtdpx->xqtc", mixed, jnp.asarray(ix).reshape(2, 2, D, pl_, nx), precision=high
    ).transpose(1, 2, 3, 0).reshape(ql, 2, cl, R, rc)
    inv = lax.all_to_all(inv.transpose(3, 0, 1, 2, 4), "rows", 0, 0, tiled=True)
    inv = inv.reshape(2 * my, cl, rc)
    spectral = jnp.einsum("kcx,ky->cxy", inv, jnp.asarray(iy), precision=high)
    act = jax.nn.gelu(
        spectral + skip_gain[:, None, None] * hidden + skip_bias[:, None, None], approximate=False
    )
    part = jnp.stack(
        [jnp.sum(project_weight[j][:, None, None] * act, axis=0) for j in range(2)]
    )
    part = part.reshape(2, rc, D, ny // D).transpose(2, 0, 1, 3)
    got = lax.all_to_all(part, "chan", 0, 0, tiled=True)
    speed = jnp.sum(got, axis=0) + project_bias[:, None, None]
    velocity = speed * ice_mask.astype(jnp.float32)[None]
    band = front_flags.astype(jnp.float32)
    W = LS_STEPS
    state = jnp.concatenate([velocity, band[None], front[None]], axis=0)
    state = with_halo(with_halo(state, "rows", 1, W), "chan", 2, W)
    u, v, bd, level = state[0], state[1], state[2], state[3]
    for step in range(LS_STEPS):
        i = step + 1
        level = advance(level, u[i:-i, i:-i], v[i:-i, i:-i], bd[i:-i, i:-i])
    return (velocity, level)


def solution(mesh):
    return jax.shard_map(
        on_device,
        mesh=mesh,
        in_specs=(
            P("chan", "rows", None),
            P("rows", "chan"),
            P(None, "rows", "chan", None, None),
            P("chan"),
            P("chan"),
            P(None, "chan"),
            P(),
            P("rows", "chan"),
            P("rows", "chan"),
        ),
        out_specs=(P(None, "rows", "chan"), P("rows", "chan")),
        check_vma=False,
    )
```

time: 345 us -> 134 us (0.39); the launches traced: 339 us -> 134 us
  waiting for transfers between devices: 132 us -> 30.2 us
  local copies, waits for them, and re-layouts: 94.8 us -> 13.5 us
  blocking collectives: 11.4 us -> 32.1 us
  matrix products: 32.5 us -> 14.2 us
  starting transfers between devices: 34.8 us -> 19.6 us
  between operations: 14.6 us -> 1.09 us
    unnamed x30 -> x26, local copies, waits for them, and re-layouts: 85.6 us -> 6.22 us
    reduce_scatter x1 -> x0, waiting for transfers between devices: 60.7 us -> none  [on_device(): lax.psum_scatter(jnp.transpose(forward_x(picked, local_tables), (1, 0, 2,...]
    all_gather x1 -> x0, waiting for transfers between devices: 39.6 us -> none  [on_device(): lax.all_gather(mixed, 'rows', axis=1, tiled=True)]
    all_to_all x0 -> x2, waiting for transfers between devices: none -> 21.8 us  [the longest x1 13.5 us: on_device(): inv = lax.all_to_all(inv.transpose(3, 0, 1, 2, 4), 'rows', 0, 0, tiled=True)]
    all_to_all x2 -> x3, blocking collectives: 11.4 us -> 32.1 us  [the longest x1 20 us: on_device(): lax.all_to_all(spec_y.reshape(R, ql, 2, cl, rc), 'rows', 0, 0, tiled=True)]
    dot_general x5 -> x4, matrix products: 32.5 us -> 14.2 us  [the longest x1 6.35 us: on_device(): spectral = jnp.einsum('kcx,ky->cxy', inv, jnp.asarray(iy), precision=high)]
    ppermute x8 -> x2, waiting for transfers between devices: 25.2 us -> 8.27 us  [with_halo(): lax.ppermute(lax.slice_in_dim(block, 0, width, axis=dim), axis, backward)]
    ppermute x8 -> x2, starting transfers between devices: 21.4 us -> 6.08 us  [with_halo(): lax.ppermute(lax.slice_in_dim(block, size - width, None, axis=dim), axis,...]
  transfers between devices with their start and end apart: 19 -> 6, of which waited for: 10 -> 5; matrix products, arithmetic and copies ran while one was open for 10% -> 0% of each run, Pallas kernels for 0% -> 0%
where the time goes in v1:
time: 134 us
  blocking collectives  32.1 us (24%)
  waiting for transfers between devices  30.2 us (23%)
  other arithmetic  22.9 us (17%)
  starting transfers between devices  19.6 us (15%)
  matrix products  14.2 us (11%)
  local copies, waits for them, and re-layouts  13.5 us (10%)
    all_to_all x1, blocking collectives, on_device(): lax.all_to_all(spec_y.reshape(R, ql, 2, cl, rc), 'rows', 0, 0, tiled=True)  20 us
    all_to_all x1, waiting for transfers between devices, on_device(): inv = lax.all_to_all(inv.transpose(3, 0, 1, 2, 4), 'rows', 0, 0, tiled=True)  13.5 us
    reduce_sum x1, other arithmetic, on_device(): jnp.sum(project_weight[j][:, None, None] * act, axis=0)  10 us
    ppermute x2, waiting for transfers between devices, with_halo(): lax.ppermute(lax.slice_in_dim(block, 0, width, axis=dim), axis, backward)  8.27 us
    all_to_all x1, waiting for transfers between devices, on_device(): got = lax.all_to_all(part, 'chan', 0, 0, tiled=True)  8.25 us
    all_to_all x1, starting transfers between devices, on_device(): inv = lax.all_to_all(inv.transpose(3, 0, 1, 2, 4), 'rows', 0, 0, tiled=True)  6.85 us
    all_to_all x1, blocking collectives, on_device(): lax.all_to_all(spec.transpose(3, 1, 2, 0, 4), 'chan', 0, 0, tiled=True)  6.37 us
    dot_general x1, matrix products, on_device(): spectral = jnp.einsum('kcx,ky->cxy', inv, jnp.asarray(iy), precision=high)  6.35 us
  transfers between devices with their start and end apart: 6, of which 5 were waited for; matrix products, arithmetic and copies ran while one was open for 0% of the time, Pallas kernels for 0%

profile of v1, /device:TPU:3, one launch (start us, length us, event | category | flops | bytes accessed | tf_op | source)
XLA Modules:
  0.0 133.7 jit_solution(18197739306992073881)
XLA Ops:
  0.6 4.7 %fusion.54 = f32[256,16,32]{0,2,1:T(8,128)S(1)} fusion(f32[256,2048,1]{1,0,2:T(8,128)} %constant.87, f32[16,32,2048]{2,1,0:T(8,128)} %param.13), kind=kOutput, calls=%fused_computation.109 | convolution fusion | flops 1610612736 | bytes 6815744 | tf_op jit(solution)/shard_map/ky,cxy->kcx/dot_general | solution.py:71
  5.3 1.3 copy.32
  6.6 0.9 reshape.54
  7.5 20.0 %all_to_all.25 = f32[16,1,8192]{2,1,0:T(1,128)S(1)} all-to-all(f32[16,1,8192]{2,1,0:T(1,128)S(1)} %reshape.54), channel_id=1, replica_groups=mesh['rows'=16,'chan'=2] {'rows'}, dimensions={0} | all-to-all | bytes 1048576 | tf_op jit(solution)/shard_map/all_to_all | solution.py:72
  27.5 0.5 broadcast.33
  28.1 1.9 %reduce.2 = f32[16,8192]{1,0:T(8,128)S(1)} reduce(f32[16,1,8192]{2,1,0:T(1,128)S(1)} %all_to_all.25, f32[]{:T(128)} %broadcast.33), dimensions={1}, to_apply=%all_to_all.15.reduce_sub_computation | reduce | bytes 1048580 | tf_op jit(solution)/shard_map/all_to_all | solution.py:72
  29.9 0.7 reshape.55
  30.6 2.7 %fusion.12 = f32[2,16,2,8,64]{4,1,0,2,3:T(8,128)S(1)} fusion(f32[2,2,64,2,16,32,1]{2,5,4,3,1,0,6:T(8,128)} %constant.88, f32[16,8,2,16,32]{4,3,2,1,0:T(8,128)S(1)} %reshape.55), kind=kOutput, calls=%fused_computation.31 | convolution fusion | flops 201326592 | bytes 1703936 | tf_op jit(solution)/shard_map/sqrcx,rsxP->qcP/dot_general | solution.py:73
  33.4 0.2 reshape.56
  33.6 6.4 %all_to_all.26 = f32[2,1,16384]{2,1,0:T(1,128)S(1)} all-to-all(f32[2,1,16384]{2,1,0:T(1,128)S(1)} %reshape.56), channel_id=1, replica_groups=mesh['rows'=16,'chan'=2] {'chan'}, dimensions={0} | all-to-all | bytes 262144 | tf_op jit(solution)/shard_map/all_to_all | solution.py:76
  40.0 1.0 reduce.3
  41.0 0.2 reshape.57
  41.2 0.2 copy.35
  41.5 4.4 %subtract_reduce_fusion = (f32[32,8,64]{2,0,1:T(8,128)S(1)}, f32[32,8,64]{2,0,1:T(8,128)S(1)}) fusion(f32[2,32,32,8,64]{4,2,1,3,0:T(8,128)} %bitcast.84, f32[32,8,64]{2,0,1:T(8,128)S(1)} %copy.37, f32[32,8,64]{2,0,1:T(8,128)S(1)} %copy.36), kind=kLoop, calls=%fused_computation.24 | loop fusion | flops 4161536 | bytes 4456448 | tf_op jit(solution)/shard_map/reduce_sum | solution.py:80
  46.1 0.2 reshape.58
  46.3 5.7 %all_to_all.27 = f32[2,1,16384]{2,1,0:T(1,128)S(1)} all-to-all(f32[2,1,16384]{2,1,0:T(1,128)S(1)} %reshape.58), channel_id=1, replica_groups=mesh['rows'=16,'chan'=2] {'chan'}, dimensions={0} | all-to-all | bytes 262144 | tf_op jit(solution)/shard_map/all_to_all | solution.py:83
  52.0 1.0 reduce.4
  53.0 0.2 reshape.59
  53.2 0.5 fusion.15
  53.7 0.5 reshape.44
  54.3 2.6 %copy.62 = f32[8,2,16,16,32]{4,2,1,0,3:T(8,128)} copy(f32[8,2,16,16,32]{4,3,0,2,1:T(8,128)S(1)} %reshape.44) | data formatting | bytes 1048576 | tf_op jit(solution)/shard_map/reshape | solution.py:86
  56.9 3.1 %reshape.60 = f32[16,1,8192]{2,1,0:T(1,128)} reshape(f32[16,8,2,16,32]{4,3,2,1,0:T(8,128)} %bitcast.83) | data formatting | bytes 1048576
  60.0 6.9 %all-to-all-start.3 = ((f32[16,1,8192]{2,1,0:T(1,128)}), f32[16,1,8192]{2,1,0:T(1,128)S(1)}, u32[]{:S(2)}, u32[]{:S(2)}) async-start(f32[16,1,8192]{2,1,0:T(1,128)} %reshape.60), calls=%async_computation.3 | async-start | bytes 1048576 | tf_op jit(solution)/shard_map/all_to_all | solution.py:87
  66.8 13.5 %all-to-all-done.3 = f32[16,1,8192]{2,1,0:T(1,128)S(1)} async-done(((f32[16,1,8192]{2,1,0:T(1,128)}), f32[16,1,8192]{2,1,0:T(1,128)S(1)}, u32[]{:S(2)}, u32[]{:S(2)}) %all-to-all-start.3) | async-done | bytes 524320 | tf_op jit(solution)/shard_map/all_to_all | solution.py:87
  80.4 1.9 %reduce.5 = f32[16,8192]{1,0:T(8,128)S(1)} reduce(f32[16,1,8192]{2,1,0:T(1,128)S(1)} %all-to-all-done.3, f32[]{:T(128)} %broadcast.33), dimensions={1}, to_apply=%all_to_all.18.reduce_sub_computation | reduce | bytes 1048580 | tf_op jit(solution)/shard_map/all_to_all | solution.py:87
  82.3 0.7 reshape.61
  83.0 6.3 %fusion.8 = (u16[32,2048]{1,0:T(8,128)(2,1)S(1)}, f32[16,32,2048]{2,1,0:T(8,128)S(1)}) fusion(f32[16]{0:T(128)S(1)} %copy-done.6, f32[16,32,2048]{2,1,0:T(8,128)} %param.13, f32[16]{0:T(128)S(1)} %copy-done.7, f32[256,2048,1]{1,0,2:T(8,128)} %constant.90, f32[256,16,32]{2,1,0:T(8,128)S(1)} %bitcast.81), kind=kOutput, calls=%fused_computation.26 | convolution fusion | flops 1621032960 | bytes 11141248 | tf_op jit(solution)/shard_map/kcx,ky->cxy/dot_general | solution.py:89
  89.4 10.0 %multiply_reduce_fusion.1 = (f32[32,2048]{1,0:T(8,128)S(1)}, f32[32,2048]{1,0:T(8,128)S(1)}) fusion(f32[16]{0:T(128)S(1)} %get-tuple-element.17, f32[16]{0:T(128)S(1)} %get-tuple-element.16, u16[32,2048]{1,0:T(8,128)(2,1)S(1)} %get-tuple-element.18, f32[16,32,2048]{2,1,0:T(8,128)S(1)} %get-tuple-element.19), kind=kLoop, calls=%fused_computation.8 | loop fusion | flops 74317824 | bytes 4849792 | tf_op jit(solution)/shard_map/reduce_sum | solution.py:94
  99.4 0.2 stack.21
  99.6 0.2 stack.22
  99.8 0.2 maximum_bitcast_fusion
  100.1 1.0 copy.43
  101.0 3.5 %all-to-all-start.4 = ((f32[2,2,32,1024]{3,2,1,0:T(8,128)}), f32[2,2,32,1024]{3,2,1,0:T(8,128)S(1)}, u32[]{:S(2)}, u32[]{:S(2)}) async-start(f32[2,2,32,1024]{3,2,1,0:T(8,128)} %copy.43), calls=%async_computation.4 | async-start | bytes 1048576 | tf_op jit(solution)/shard_map/all_to_all | solution.py:97
  104.6 8.3 %all-to-all-done.4 = f32[2,2,32,1024]{3,2,1,0:T(8,128)S(1)} async-done(((f32[2,2,32,1024]{3,2,1,0:T(8,128)}), f32[2,2,32,1024]{3,2,1,0:T(8,128)S(1)}, u32[]{:S(2)}, u32[]{:S(2)}) %all-to-all-start.4) | async-done | bytes 524320 | tf_op jit(solution)/shard_map/all_to_all | solution.py:97
  112.9 0.1 add_multiply_fusion
  113.0 4.2 %collective-permute-start = (f32[4,4,1024]{2,1,0:T(4,128)S(1)}, f32[4,4,1024]{2,1,0:T(4,128)S(1)}, u32[]{:S(2)}, u32[]{:S(2)}) collective-permute-start(f32[4,4,1024]{2,1,0:T(4,128)S(1)} %get-tuple-element.12), channel_id=1, source_target_pairs={{0,2},{2,4},{4,6},{6,8},{8,10},{10,12},{12,14},{14,16},{16,18},{18... | collective-permute-start | bytes 196616 | tf_op jit(solution)/shard_map/ppermute | solution.py:23
  117.2 1.9 %collective-permute-start.1 = (f32[4,4,1024]{2,1,0:T(4,128)S(1)}, f32[4,4,1024]{2,1,0:T(4,128)S(1)}, u32[]{:S(2)}, u32[]{:S(2)}) collective-permute-start(f32[4,4,1024]{2,1,0:T(4,128)S(1)} %get-tuple-element.13), channel_id=1, source_target_pairs={{2,0},{4,2},{6,4},{8,6},{10,8},{12,10},{14,12},{16,14},{18,16},{20... | collective-permute-start | bytes 196616 | tf_op jit(solution)/shard_map/ppermute | solution.py:24
  119.1 4.5 %collective-permute-done.1 = f32[4,4,1024]{2,1,0:T(4,128)S(1)} collective-permute-done((f32[4,4,1024]{2,1,0:T(4,128)S(1)}, f32[4,4,1024]{2,1,0:T(4,128)S(1)}, u32[]{:S(2)}, u32[]{:S(2)}) %collective-permute-start.1) | collective-permute-done | bytes 65568 | tf_op jit(solution)/shard_map/ppermute | solution.py:24
  123.7 0.1 pad_maximum_fusion
  123.9 1.9 %collective-permute-start.2 = (f32[4,40,4]{2,1,0:T(8,128)S(1)}, f32[4,40,4]{2,1,0:T(8,128)S(1)}, u32[]{:S(2)}, u32[]{:S(2)}) collective-permute-start(f32[4,40,4]{2,1,0:T(8,128)S(1)} %get-tuple-element.11), channel_id=1, source_target_pairs={{0,1},{2,3},{4,5},{6,7},{8,9},{10,11},{12,13},{14,15},{16,17},{18,... | collective-permute-start | bytes 7688 | tf_op jit(solution)/shard_map/ppermute | solution.py:23
  125.8 1.3 collective-permute-start.3
  127.1 0.2 collective-permute-done.2
  127.3 3.7 %collective-permute-done.3 = f32[4,40,4]{2,1,0:T(8,128)S(1)} collective-permute-done((f32[4,40,4]{2,1,0:T(8,128)S(1)}, f32[4,40,4]{2,1,0:T(8,128)S(1)}, u32[]{:S(2)}, u32[]{:S(2)}) %collective-permute-start.3) | collective-permute-done | bytes 2592 | tf_op jit(solution)/shard_map/ppermute | solution.py:24
  131.0 0.4 concatenate.13
  131.5 0.4 fusion.38
  131.9 0.4 fusion.29
  132.3 0.4 fusion.20
  132.7 1.0 fusion.47
  (35 shorter events, 0.6 us)
Async XLA Ops:
  41.5 11.8 %copy-start.1 = (f32[2,2,2,64,512,1]{4,3,0,1,5,2:T(8,128)S(1)}, f32[2,2,2,64,512,1]{4,3,0,1,5,2:T(8,128)}, u32[]{:S(2)}) copy-start(f32[2,2,2,64,512,1]{4,3,0,1,5,2:T(8,128)} %constant.89) | copy-start | bytes 3145732
  54.3 12.6 %copy-start.5 = (f32[2,16]{1,0:T(2,128)S(1)}, f32[2,16]{1,0:T(2,128)}, u32[]{:S(2)}) copy-start(f32[2,16]{1,0:T(2,128)} %param.18) | copy-start | bytes 388
  56.8 26.1 %copy-start.6 = (f32[16]{0:T(128)S(1)}, f32[16]{0:T(128)}, u32[]{:S(2)}) copy-start(f32[16]{0:T(128)} %param.17) | copy-start | bytes 196
  56.9 26.1 %copy-start.7 = (f32[16]{0:T(128)S(1)}, f32[16]{0:T(128)}, u32[]{:S(2)}) copy-start(f32[16]{0:T(128)} %param.16) | copy-start | bytes 196
  60.0 20.4 %all-to-all-start.3 = ((f32[16,1,8192]{2,1,0:T(1,128)}), f32[16,1,8192]{2,1,0:T(1,128)S(1)}, u32[]{:S(2)}, u32[]{:S(2)}) async-start(f32[16,1,8192]{2,1,0:T(1,128)} %reshape.60), calls=%async_computation.3 | async-start | bytes 1048576 | tf_op jit(solution)/shard_map/all_to_all | solution.py:87
  89.3 15.2 %copy-start.3 = (s32[32,1024]{1,0:T(8,128)S(1)}, s32[32,1024]{1,0:T(8,128)}, u32[]{:S(2)}) copy-start(s32[32,1024]{1,0:T(8,128)} %param.20) | copy-start | bytes 393220
  89.4 15.2 %copy-start.4 = (s32[32,1024]{1,0:T(8,128)S(1)}, s32[32,1024]{1,0:T(8,128)}, u32[]{:S(2)}) copy-start(s32[32,1024]{1,0:T(8,128)} %param.21) | copy-start | bytes 393220
  89.4 23.5 %copy-start.8 = (f32[2]{0:T(128)S(1)}, f32[2]{0:T(128)}, u32[]{:S(2)}) copy-start(f32[2]{0:T(128)} %param.19) | copy-start | bytes 28
  99.4 13.6 %copy-start.2 = (f32[32,1024]{1,0:T(8,128)S(1)}, f32[32,1024]{1,0:T(8,128)}, u32[]{:S(2)}) copy-start(f32[32,1024]{1,0:T(8,128)} %param.14) | copy-start | bytes 393220
  101.0 11.8 %all-to-all-start.4 = ((f32[2,2,32,1024]{3,2,1,0:T(8,128)}), f32[2,2,32,1024]{3,2,1,0:T(8,128)S(1)}, u32[]{:S(2)}, u32[]{:S(2)}) async-start(f32[2,2,32,1024]{3,2,1,0:T(8,128)} %copy.43), calls=%async_computation.4 | async-start | bytes 1048576 | tf_op jit(solution)/shard_map/all_to_all | solution.py:97
  113.0 19.3 %copy-start = (f32[2,32,1024]{2,1,0:T(8,128)}, f32[2,32,1024]{2,1,0:T(8,128)S(1)}, u32[]{:S(2)}) copy-start(f32[2,32,1024]{2,1,0:T(8,128)S(1)} %add_multiply_fusion) | copy-start | bytes 786436
  113.0 6.1 %collective-permute-start = (f32[4,4,1024]{2,1,0:T(4,128)S(1)}, f32[4,4,1024]{2,1,0:T(4,128)S(1)}, u32[]{:S(2)}, u32[]{:S(2)}) collective-permute-start(f32[4,4,1024]{2,1,0:T(4,128)S(1)} %get-tuple-element.12), channel_id=1, source_target_pairs={{0,2},{2,4},{4,6},{6,8},{8,10},{10,12},{12,14},{14,16},{16,18},{18... | collective-permute-start | bytes 196616 | tf_op jit(solution)/shard_map/ppermute | solution.py:23
  117.2 6.5 %collective-permute-start.1 = (f32[4,4,1024]{2,1,0:T(4,128)S(1)}, f32[4,4,1024]{2,1,0:T(4,128)S(1)}, u32[]{:S(2)}, u32[]{:S(2)}) collective-permute-start(f32[4,4,1024]{2,1,0:T(4,128)S(1)} %get-tuple-element.13), channel_id=1, source_target_pairs={{2,0},{4,2},{6,4},{8,6},{10,8},{12,10},{14,12},{16,14},{18,16},{20... | collective-permute-start | bytes 196616 | tf_op jit(solution)/shard_map/ppermute | solution.py:24
  123.9 3.4 %collective-permute-start.2 = (f32[4,40,4]{2,1,0:T(8,128)S(1)}, f32[4,40,4]{2,1,0:T(8,128)S(1)}, u32[]{:S(2)}, u32[]{:S(2)}) collective-permute-start(f32[4,40,4]{2,1,0:T(8,128)S(1)} %get-tuple-element.11), channel_id=1, source_target_pairs={{0,1},{2,3},{4,5},{6,7},{8,9},{10,11},{12,13},{14,15},{16,17},{18,... | collective-permute-start | bytes 7688 | tf_op jit(solution)/shard_map/ppermute | solution.py:23
  125.8 5.2 %collective-permute-start.3 = (f32[4,40,4]{2,1,0:T(8,128)S(1)}, f32[4,40,4]{2,1,0:T(8,128)S(1)}, u32[]{:S(2)}, u32[]{:S(2)}) collective-permute-start(f32[4,40,4]{2,1,0:T(8,128)S(1)} %get-tuple-element.10), channel_id=1, source_target_pairs={{1,0},{3,2},{5,4},{7,6},{9,8},{11,10},{13,12},{15,14},{17,16},{19,... | collective-permute-start | bytes 7688 | tf_op jit(solution)/shard_map/ppermute | solution.py:24

commit v2 on v1

--- a/solution.py
+++ b/solution.py
@@ -4,6 +4,8 @@
 import jax.numpy as jnp
 import numpy as np
 from jax import lax
+from jax.experimental import pallas as pl
+from jax.experimental.pallas import tpu as pltpu
 from jax.sharding import PartitionSpec as P
 
 LS_STEPS = 4
@@ -34,6 +36,360 @@
     transport = jnp.maximum(u, 0.0) * back_x + jnp.minimum(u, 0.0) * ahead_x
     transport = transport + jnp.maximum(v, 0.0) * back_y + jnp.minimum(v, 0.0) * ahead_y
     return center - time_step * band * transport
+
+
+MESH = pl.DeviceIdType.MESH
+f32 = jnp.float32
+NT = (((1,), (1,)), ((), ()))
+NN = (((1,), (0,)), ((), ()))
+CW = 256
+
+
+def split(x):
+    hi = x.astype(jnp.bfloat16)
+    return hi, (x - hi.astype(f32)).astype(jnp.bfloat16)
+
+
+def np_split(x):
+    x = x.astype(np.float32)
+    hi = x.astype(jnp.bfloat16)
+    lo = (x - hi.astype(np.float32)).astype(jnp.bfloat16)
+    return jnp.asarray(hi), jnp.asarray(lo)
+
+
+def dot3(a, b, dims):
+    def one(x, y):
+        return lax.dot_general(x, y, dims, preferred_element_type=f32)
+
+    return one(a[0], b[0]) + (one(a[0], b[1]) + one(a[1], b[0]))
+
+
+def spread(R, me, src, dst, send, recv):
+    chan = lax.axis_index("chan")
+    copies = []
+    for step in range(1, R):
+        to = lax.rem(me + step, R)
+        copies.append(
+            pltpu.make_async_remote_copy(
+                src_ref=src.at[to],
+                dst_ref=dst.at[me],
+                send_sem=send.at[step],
+                recv_sem=recv.at[step],
+                device_id=(to, chan),
+                device_id_type=MESH,
+            )
+        )
+    return copies
+
+
+def greet(R, me, chan):
+    barrier = pltpu.get_barrier_semaphore()
+    for step in range(1, R):
+        pl.semaphore_signal(
+            barrier, inc=1, device_id=(lax.rem(me + step, R), chan), device_id_type=MESH
+        )
+    pl.semaphore_signal(barrier, inc=1, device_id=(me, 1 - chan), device_id_type=MESH)
+    return barrier
+
+
+def forward_kernel(R, hid, fyh, fyl, txh, txl, out, spec, got, xs, chs, chr_, ssem, rsem, csem):
+    me = lax.axis_index("rows")
+    chan = lax.axis_index("chan")
+    cl, rc, ny = hid.shape
+    barrier = greet(R, me, chan)
+    acc = jnp.zeros((fyh.shape[0], cl * rc), f32)
+    kc = 512
+    for j in range(ny // kc):
+        cols = slice(j * kc, (j + 1) * kc)
+        h = split(hid[:, :, cols].reshape(cl * rc, kc))
+        acc = acc + dot3((fyh[:, cols], fyl[:, cols]), h, NT)
+    spec[...] = acc.reshape(spec.shape)
+    pl.semaphore_wait(barrier, R)
+    copies = spread(R, me, spec, got, ssem, rsem)
+    for copy in copies:
+        copy.start()
+    got[me] = spec[me]
+    for copy in copies:
+        copy.wait()
+    half = cl * 8
+    for ri in range(2):
+        for c in range(cl):
+            xs[ri * half + c * 8 : ri * half + c * 8 + 8, :] = jnp.concatenate(
+                [got[s, ri * 8 : ri * 8 + 8, c * rc : (c + 1) * rc] for s in range(R)], axis=1
+            )
+    g = dot3((txh[...], txl[...]), split(xs[...]), NT)
+    mx = g.shape[0] // 2
+    re = g[:mx, :half] + g[mx:, half:]
+    im = g[:mx, half:] - g[mx:, :half]
+    hp = mx // 2
+    for d in range(2):
+        chs[d, 0] = re[d * hp : (d + 1) * hp]
+        chs[d, 1] = im[d * hp : (d + 1) * hp]
+    copy = pltpu.make_async_remote_copy(
+        src_ref=chs.at[1 - chan],
+        dst_ref=chr_,
+        send_sem=csem.at[0],
+        recv_sem=csem.at[1],
+        device_id=(me, 1 - chan),
+        device_id_type=MESH,
+    )
+    copy.start()
+    out[chan] = chs[chan]
+    copy.wait()
+    out[1 - chan] = chr_[...]
+
+
+def inverse_kernel(
+    R, hid, mixd, tih, til, iyh, iyl, gain, bias, pw, pb, mask, front, flags,
+    vel, nxt,
+    mall, chr_, isrc, igot, xs, xth, xtl, spc, psend, pgot, own, phi, ab,
+    ssem, rsem, csem, psem, qsem, hs, hr,
+):
+    me = lax.axis_index("rows")
+    chan = lax.axis_index("chan")
+    cl, rc, ny = hid.shape
+    half = cl * 8
+    tw = ny // 2
+    nch = tw // CW
+    last = R - 1
+    phi[...] = jnp.zeros_like(phi)
+    ab[...] = jnp.zeros_like(ab)
+    phi[8 : 8 + rc, 128 : 128 + tw] = front[...]
+    barrier = greet(R, me, chan)
+
+    for step in (1, R - 1):
+        pl.semaphore_signal(
+            barrier, inc=1, device_id=(lax.rem(me + step, R), 1 - chan), device_id_type=MESH
+        )
+    pl.semaphore_wait(barrier, R + 2)
+
+    ccopy = pltpu.make_async_remote_copy(
+        src_ref=mixd.at[1 - chan],
+        dst_ref=chr_,
+        send_sem=csem.at[0],
+        recv_sem=csem.at[1],
+        device_id=(me, 1 - chan),
+        device_id_type=MESH,
+    )
+    ccopy.start()
+
+    csrc = pl.multiple_of(tw - (tw - 128) * chan, 128)
+    cdst = pl.multiple_of((tw + 128) * chan, 128)
+    mid = (pl.ds(128, tw), pl.ds(128, tw))
+    side = (pl.ds(csrc, 128), pl.ds(cdst, 128))
+    up = (pl.ds(8, 8), pl.ds(8 + rc, 8))
+    down = (pl.ds(rc, 8), pl.ds(0, 8))
+    level = (pl.ds(8, rc), pl.ds(8, rc))
+    moves = [(-1, 0, up, mid), (1, 0, down, mid), (0, 1, level, side), (-1, 1, up, side), (1, 1, down, side)]
+
+    def halo(which, ref, act):
+        for n, (dr, dc, rows, cols) in enumerate(moves):
+            i = which * 5 + n
+            lead = () if which == 0 else (slice(None),)
+            copy = pltpu.make_async_remote_copy(
+                src_ref=ref.at[lead + (rows[0], cols[0])],
+                dst_ref=ref.at[lead + (rows[1], cols[1])],
+                send_sem=hs.at[i],
+                recv_sem=hr.at[i],
+                device_id=(me + dr, 1 - chan if dc else chan),
+                device_id_type=MESH,
+            )
+            first = (lambda: copy.start()) if act == "start" else (lambda: copy.wait_send())
+            if dr == 0:
+                first()
+                if act == "wait":
+                    copy.wait_recv()
+            else:
+                pl.when(me > 0 if dr < 0 else me < last)(first)
+                if act == "wait":
+                    pl.when(me < last if dr < 0 else me > 0)(lambda: copy.wait_recv())
+
+    halo(0, phi, "start")
+
+    mall[chan] = mixd[chan]
+    ccopy.wait()
+    mall[1 - chan] = chr_[...]
+    re = jnp.concatenate([mall[0, 0], mall[1, 0]], axis=0)
+    im = jnp.concatenate([mall[0, 1], mall[1, 1]], axis=0)
+    full = jnp.concatenate(
+        [jnp.concatenate([re, im], axis=1), jnp.concatenate([-im, re], axis=1)], axis=0
+    )
+    res = dot3((tih[...], til[...]), split(full), NN)
+    isrc[...] = res.reshape(isrc.shape)
+    copies = spread(R, me, isrc, igot, ssem, rsem)
+    for copy in copies:
+        copy.start()
+    igot[me] = isrc[me]
+    for copy in copies:
+        copy.wait()
+    for s in range(R):
+        t = igot[s].T
+        for ri in range(2):
+            xs[s * 16 + ri * 8 : s * 16 + ri * 8 + 8, :] = jnp.concatenate(
+                [t[ri * half + c * 8 : ri * half + c * 8 + 8, :] for c in range(cl)], axis=1
+            )
+    xt = split(xs[...].T)
+    xth[...] = xt[0]
+    xtl[...] = xt[1]
+
+    def share(col):
+        cols = pl.ds(pl.multiple_of(col, CW), CW)
+        spc[...] = dot3((xth[...], xtl[...]), (iyh[:, cols], iyl[:, cols]), NN)
+        u = jnp.zeros((rc, CW), f32)
+        v = jnp.zeros((rc, CW), f32)
+        for c in range(cl):
+            z = spc[c * rc : (c + 1) * rc, :] + (gain[c] * hid[c, :, cols] + bias[c])
+            a = (0.5 * z) * (1.0 + lax.erf(z * (0.5**0.5)))
+            u = u + pw[0, c] * a
+            v = v + pw[1, c] * a
+        return u, v
+
+    def pcopy(j):
+        return pltpu.make_async_remote_copy(
+            src_ref=psend.at[j],
+            dst_ref=pgot.at[j],
+            send_sem=psem.at[j],
+            recv_sem=qsem.at[j],
+            device_id=(me, 1 - chan),
+            device_id_type=MESH,
+        )
+
+    def theirs(j, carry):
+        u, v = share((1 - chan) * tw + j * CW)
+        psend[j, 0] = u
+        psend[j, 1] = v
+        pcopy(j).start()
+        return carry
+
+    def ours(j, carry):
+        u, v = share(chan * tw + j * CW)
+        own[j, 0] = u
+        own[j, 1] = v
+        return carry
+
+    lax.fori_loop(0, nch, theirs, 0)
+    lax.fori_loop(0, nch, ours, 0)
+    for j in range(nch):
+        pcopy(j).wait()
+        cols = slice(j * CW, (j + 1) * CW)
+        ice = mask[:, cols].astype(f32)
+        band = flags[:, cols].astype(f32) * time_step
+        for k in range(2):
+            w = (own[j, k] + pgot[j, k] + pb[k]) * ice
+            vel[k, :, cols] = w
+            ab[k, 8 : 8 + rc, 128 + j * CW : 128 + (j + 1) * CW] = w * band
+    halo(1, ab, "start")
+    halo(0, phi, "wait")
+    halo(1, ab, "wait")
+    a = ab[0]
+    b = ab[1]
+    ap, am = jnp.maximum(a, 0.0), jnp.minimum(a, 0.0)
+    bp, bm = jnp.maximum(b, 0.0), jnp.minimum(b, 0.0)
+    x = phi[...]
+    nr, nc = x.shape
+    for _ in range(LS_STEPS):
+        move = ap * (x - pltpu.roll(x, 1, 0)) + am * (pltpu.roll(x, nr - 1, 0) - x)
+        move = move + (bp * (x - pltpu.roll(x, 1, 1)) + bm * (pltpu.roll(x, nc - 1, 1) - x))
+        x = x - move
+    nxt[...] = x[8 : 8 + rc, 128 : 128 + tw]
+
+
+def on_kernels(
+    hidden, front, spectral_weight, skip_gain, skip_bias, project_weight, project_bias,
+    ice_mask, front_flags,
+):
+    cl, rc, ny = hidden.shape
+    R = lax.axis_size("rows")
+    D = lax.axis_size("chan")
+    ql = spectral_weight.shape[1]
+    pn = spectral_weight.shape[2]
+    nx, mx, my = rc * R, pn * D, ql * R
+    scale = 1.0 / math.sqrt(nx * ny * mx * my)
+    yph = np_angles(np.arange(my), np.arange(ny), ny).reshape(R, ql, ny)
+    fy = np.stack([np.cos(yph), -np.sin(yph)], axis=1).reshape(2 * my, ny)
+    w = np.where(np.arange(my) == 0, 1.0, 2.0).reshape(R, ql, 1) * scale
+    iy = np.stack([w * np.cos(yph), -w * np.sin(yph)], axis=1).reshape(2 * my, ny)
+    pid = np.arange(mx)
+    xph = np_angles(np.where(pid < mx // 2, pid, pid - mx), np.arange(nx), nx)
+    tx = np.concatenate([np.cos(xph), np.sin(xph)], axis=0)
+    vm = pl.BlockSpec(memory_space=pltpu.VMEM)
+    sm = pl.BlockSpec(memory_space=pltpu.SMEM)
+    dma = pltpu.SemaphoreType.DMA
+    lanes = cl * ql
+
+    def kernel_a(*refs):
+        forward_kernel(R, *refs)
+
+    def kernel_b(*refs):
+        inverse_kernel(R, *refs)
+
+    spec = pl.pallas_call(
+        kernel_a,
+        out_shape=jax.ShapeDtypeStruct((D, 2, pn, lanes), f32),
+        in_specs=[vm] * 5,
+        out_specs=vm,
+        scratch_shapes=[
+            pltpu.VMEM((R, 2 * ql, cl * rc), f32),
+            pltpu.VMEM((R, 2 * ql, cl * rc), f32),
+            pltpu.VMEM((2 * lanes, nx), f32),
+            pltpu.VMEM((D, 2, pn, lanes), f32),
+            pltpu.VMEM((2, pn, lanes), f32),
+            dma((R,)),
+            dma((R,)),
+            dma((2,)),
+        ],
+        compiler_params=pltpu.CompilerParams(
+            collective_id=0, has_side_effects=True, vmem_limit_bytes=40 * 2**20
+        ),
+        name="forward",
+    )(hidden, *np_split(fy), *np_split(tx))
+    spec = spec.reshape(D, 2, pn, cl, ql).transpose(1, 0, 3, 4, 2).reshape(2, D * cl, ql, pn)
+    wt = spectral_weight.transpose(0, 3, 4, 1, 2)
+    a, b = spec[0][:, None], spec[1][:, None]
+    re = jnp.sum(wt[0] * a - wt[1] * b, axis=0)
+    im = jnp.sum(wt[0] * b + wt[1] * a, axis=0)
+    mixed = jnp.stack([re, im]).reshape(2, D, cl, ql, pn).transpose(1, 0, 4, 2, 3)
+    mixed = mixed.reshape(D, 2, pn, lanes)
+    nch = ny // D // CW
+    tw = ny // D
+    return pl.pallas_call(
+        kernel_b,
+        out_shape=(
+            jax.ShapeDtypeStruct((2, rc, tw), f32),
+            jax.ShapeDtypeStruct((rc, tw), f32),
+        ),
+        in_specs=[vm] * 6 + [sm] * 4 + [vm] * 3,
+        out_specs=(vm, vm),
+        scratch_shapes=[
+            pltpu.VMEM((D, 2, pn, lanes), f32),
+            pltpu.VMEM((2, pn, lanes), f32),
+            pltpu.VMEM((R, rc, 2 * lanes), f32),
+            pltpu.VMEM((R, rc, 2 * lanes), f32),
+            pltpu.VMEM((2 * my, cl * rc), f32),
+            pltpu.VMEM((cl * rc, 2 * my), jnp.bfloat16),
+            pltpu.VMEM((cl * rc, 2 * my), jnp.bfloat16),
+            pltpu.VMEM((cl * rc, CW), f32),
+            pltpu.VMEM((nch, 2, rc, CW), f32),
+            pltpu.VMEM((nch, 2, rc, CW), f32),
+            pltpu.VMEM((nch, 2, rc, CW), f32),
+            pltpu.VMEM((rc + 16, tw + 256), f32),
+            pltpu.VMEM((2, rc + 16, tw + 256), f32),
+            dma((R,)),
+            dma((R,)),
+            dma((2,)),
+            dma((nch,)),
+            dma((nch,)),
+            dma((10,)),
+            dma((10,)),
+        ],
+        compiler_params=pltpu.CompilerParams(
+            collective_id=1, has_side_effects=True, vmem_limit_bytes=40 * 2**20
+        ),
+        name="inverse",
+    )(
+        hidden, mixed, *np_split(tx.T), *np_split(iy), skip_gain, skip_bias,
+        project_weight, project_bias, ice_mask, front, front_flags,
+    )
 
 
 def on_device(
@@ -51,6 +407,11 @@
     R = lax.axis_size("rows")
     D = lax.axis_size("chan")
     ql = spectral_weight.shape[1]
+    if D == 2 and ql == 8 and cl * ql == 128 and rc % 8 == 0 and (rc * R) % 128 == 0:
+        return on_kernels(
+            hidden, front, spectral_weight, skip_gain, skip_bias, project_weight,
+            project_bias, ice_mask, front_flags,
+        )
     pl_ = spectral_weight.shape[2]
     nx = rc * R
     mx = pl_ * D

time: 134 us -> 71.9 us (0.54)
  Pallas kernels: 0 us -> 54.7 us
  blocking collectives: 32.1 us -> 0 us
  waiting for transfers between devices: 30.2 us -> 0 us
  starting transfers between devices: 19.6 us -> 0 us
  other arithmetic: 22.9 us -> 4.48 us
  matrix products: 14.2 us -> 0 us
  local copies, waits for them, and re-layouts: 13.5 us -> 10.6 us
    pallas_call x0 -> x2, Pallas kernels: none -> 54.7 us  [the longest x1 34.9 us: on_kernels(): pl.pallas_call(kernel_b, out_shape=(jax.ShapeDtypeStruct((2, rc, tw), f32...]
    all_to_all x3 -> x0, blocking collectives: 32.1 us -> none  [the longest x1 20 us: on_device(): lax.all_to_all(spec_y.reshape(R, ql, 2, cl, rc), 'rows', 0, 0, tiled=True)]
    all_to_all x2 -> x0, waiting for transfers between devices: 21.8 us -> none  [the longest x1 13.5 us: on_device(): inv = lax.all_to_all(inv.transpose(3, 0, 1, 2, 4), 'rows', 0, 0, tiled=True)]
    dot_general x4 -> x0, matrix products: 14.2 us -> none  [the longest x1 6.35 us: on_device(): spectral = jnp.einsum('kcx,ky->cxy', inv, jnp.asarray(iy), precision=high)]
    all_to_all x2 -> x0, starting transfers between devices: 10.3 us -> none  [the longest x1 6.85 us: on_device(): inv = lax.all_to_all(inv.transpose(3, 0, 1, 2, 4), 'rows', 0, 0, tiled=True)]
    reduce_sum x3 -> x1, other arithmetic: 14.4 us -> 4.45 us  [on_kernels(): re = jnp.sum(wt[0] * a - wt[1] * b, axis=0)]
    ppermute x4 -> x0, starting transfers between devices: 9.29 us -> none  [the longest x2 6.08 us: with_halo(): lax.ppermute(lax.slice_in_dim(block, size - width, None, axis=dim), axis,...]
    ppermute x4 -> x0, waiting for transfers between devices: 8.43 us -> none  [the longest x2 8.27 us: with_halo(): lax.ppermute(lax.slice_in_dim(block, 0, width, axis=dim), axis, backward)]
  transfers between devices with their start and end apart: 6 -> 0, of which waited for: 5 -> 0; matrix products, arithmetic and copies ran while one was open for 0% -> 0% of each run, Pallas kernels for 0% -> 0%
where the time goes in v2:
time: 71.9 us; the launch traced here: 70.7 us
  Pallas kernels  54.7 us (76%)
  local copies, waits for them, and re-layouts  10.6 us (15%)
  other arithmetic  4.48 us (6%)
  between operations  0.91 us (1%)
    pallas_call x1, Pallas kernels, on_kernels(): pl.pallas_call(kernel_b, out_shape=(jax.ShapeDtypeStruct((2, rc, tw), f32...  34.9 us
    pallas_call x1, Pallas kernels, on_kernels(): pl.pallas_call(kernel_a, out_shape=jax.ShapeDtypeStruct((D, 2, pn, lanes)...  19.8 us
    unnamed x36, local copies, waits for them, and re-layouts  10.1 us
    reduce_sum x1, other arithmetic, on_kernels(): re = jnp.sum(wt[0] * a - wt[1] * b, axis=0)  4.45 us

profile of v2, /device:TPU:3, one launch (start us, length us, event | category | flops | bytes accessed | tf_op | source)
XLA Modules:
  0.0 70.7 jit_solution(15246067179040578142)
XLA Ops:
  0.6 0.0 copy-start
  0.6 2.2 %copy-done = f32[16,32,2048]{2,1,0:T(8,128)S(1)} copy-done((f32[16,32,2048]{2,1,0:T(8,128)S(1)}, f32[16,32,2048]{2,1,0:T(8,128)}, u32[]{:S(2)}) %copy-start) | copy-done | bytes 4194328
  2.8 0.0 copy-start.4
  2.8 1.2 %copy-done.4 = bf16[256,2048]{1,0:T(8,128)(2,1)S(1)} copy-done((bf16[256,2048]{1,0:T(8,128)(2,1)S(1)}, bf16[256,2048]{1,0:T(8,128)(2,1)}, u32[]{:S(2)}) %copy-start.4) | copy-done | bytes 1048600
  4.0 0.0 copy-start.5
  4.0 1.2 %copy-done.5 = bf16[256,2048]{1,0:T(8,128)(2,1)S(1)} copy-done((bf16[256,2048]{1,0:T(8,128)(2,1)S(1)}, bf16[256,2048]{1,0:T(8,128)(2,1)}, u32[]{:S(2)}) %copy-start.5) | copy-done | bytes 1048600
  5.3 0.0 copy-start.8
  5.3 0.9 %copy-done.8 = bf16[256,512]{1,0:T(8,128)(2,1)S(1)} copy-done((bf16[256,512]{1,0:T(8,128)(2,1)S(1)}, bf16[256,512]{1,0:T(8,128)(2,1)}, u32[]{:S(2)}) %copy-start.8) | copy-done | bytes 262168
  6.2 0.0 copy-start.9
  6.2 0.9 %copy-done.9 = bf16[256,512]{1,0:T(8,128)(2,1)S(1)} copy-done((bf16[256,512]{1,0:T(8,128)(2,1)S(1)}, bf16[256,512]{1,0:T(8,128)(2,1)}, u32[]{:S(2)}) %copy-start.9) | copy-done | bytes 262168
  7.2 19.8 %forward.1 = f32[2,2,64,128]{3,2,1,0:T(8,128)S(1)} custom-call(f32[16,32,2048]{2,1,0:T(8,128)S(1)} %copy-done, bf16[256,2048]{1,0:T(8,128)(2,1)S(1)} %copy-done.5, bf16[256,2048]{1,0:T(8,128)(2,1)S(1)} %copy-done.4, bf16[256,512]{1,0:T(8,128)(2,1)S(1)} %copy-done.9, bf16[256,512]{1,0:T(8,128)(2,1)S(1)} %copy-done.8), custom_call_target="tpu_custom_call" | custom-call | tf_op jit(solution)/shard_map/forward/pallas_call | solution.py:326
  27.0 0.1 copy.24
  27.2 0.0 copy-start.2
  27.3 0.0 copy-start.3
  27.3 0.0 copy-start.6
  27.3 0.0 copy-start.7
  27.3 0.0 copy-start.10
  27.3 0.0 copy-start.11
  27.3 0.0 copy-start.12
  27.3 0.0 copy-start.13
  27.3 0.0 copy-start.14
  27.3 0.0 copy-start.15
  27.4 0.0 copy-start.16
  27.4 4.5 %subtract_reduce_fusion = (f32[32,8,64]{2,0,1:T(8,128)S(1)}, f32[32,8,64]{2,0,1:T(8,128)S(1)}) fusion(f32[2,32,32,8,64]{4,2,1,3,0:T(8,128)} %bitcast.24, f32[32,8,64]{2,0,1:T(8,128)S(1)} %copy.26, f32[32,8,64]{2,0,1:T(8,128)S(1)} %copy.25), kind=kLoop, calls=%fused_computation.3 | loop fusion | flops 4161536 | bytes 4456448 | tf_op jit(solution)/shard_map/reduce_sum | solution.py:349
  31.8 0.1 copy.27
  31.9 0.1 copy.28
  32.0 0.1 copy.30.refs_1_
  32.2 0.0 copy-done.2
  32.2 0.0 copy-done.3
  32.2 0.0 copy-done.6
  32.2 0.0 copy-done.7
  32.2 0.0 copy-done.10
  32.2 0.0 copy-done.11
  32.2 0.0 copy-done.12
  32.2 0.0 copy-done.13
  32.2 0.0 copy-done.14
  32.2 0.0 copy-done.15
  32.3 0.0 copy-done.16
  32.3 0.0 copy-start.1
  32.3 2.2 %copy-done.1 = f32[16,32,2048]{2,1,0:T(8,128)S(1)} copy-done((f32[16,32,2048]{2,1,0:T(8,128)S(1)}, f32[16,32,2048]{2,1,0:T(8,128)}, u32[]{:S(2)}) %copy-start.1) | copy-done | bytes 4194328
  34.5 34.9 %inverse.1 = (f32[2,32,1024]{2,1,0:T(8,128)S(1)}, f32[32,1024]{1,0:T(8,128)S(1)}) custom-call(f32[16,32,2048]{2,1,0:T(8,128)S(1)} %copy-done.1, f32[2,2,64,128]{3,2,1,0:T(8,128)S(1)} %copy.30.refs_1_, bf16[512,256]{1,0:T(8,128)(2,1)S(1)} %copy-done.7, bf16[512,256]{1,0:T(8,128)(2,1)S(1)} %copy-done.6, bf16[256,2048]{1,0:T(8,128)(2,1)S(1)} %copy-done.3, ...), custom_call_target="tpu_custom_call" | custom-call | tf_op jit(solution)/shard_map/inverse/pallas_call | solution.py:355
  69.4 0.7 copy.35
  70.1 0.7 copy.36
  (4 shorter events, 0.1 us)
Async XLA Ops:
  0.6 2.2 %copy-start = (f32[16,32,2048]{2,1,0:T(8,128)S(1)}, f32[16,32,2048]{2,1,0:T(8,128)}, u32[]{:S(2)}) copy-start(f32[16,32,2048]{2,1,0:T(8,128)} %refs_0_.3) | copy-start | bytes 12582916
  2.8 1.2 %copy-start.4 = (bf16[256,2048]{1,0:T(8,128)(2,1)S(1)}, bf16[256,2048]{1,0:T(8,128)(2,1)}, u32[]{:S(2)}) copy-start(bf16[256,2048]{1,0:T(8,128)(2,1)} %constant.19.clone.refs_2_) | copy-start | bytes 3145732
  4.0 1.2 %copy-start.5 = (bf16[256,2048]{1,0:T(8,128)(2,1)S(1)}, bf16[256,2048]{1,0:T(8,128)(2,1)}, u32[]{:S(2)}) copy-start(bf16[256,2048]{1,0:T(8,128)(2,1)} %constant.18.clone.refs_1_) | copy-start | bytes 3145732
  5.3 0.9 %copy-start.8 = (bf16[256,512]{1,0:T(8,128)(2,1)S(1)}, bf16[256,512]{1,0:T(8,128)(2,1)}, u32[]{:S(2)}) copy-start(bf16[256,512]{1,0:T(8,128)(2,1)} %constant.21.clone.refs_4_) | copy-start | bytes 786436
  6.2 0.9 %copy-start.9 = (bf16[256,512]{1,0:T(8,128)(2,1)S(1)}, bf16[256,512]{1,0:T(8,128)(2,1)}, u32[]{:S(2)}) copy-start(bf16[256,512]{1,0:T(8,128)(2,1)} %constant.20.clone.refs_3_) | copy-start | bytes 786436
  27.2 4.9 %copy-start.2 = (bf16[256,2048]{1,0:T(8,128)(2,1)S(1)}, bf16[256,2048]{1,0:T(8,128)(2,1)}, u32[]{:S(2)}) copy-start(bf16[256,2048]{1,0:T(8,128)(2,1)} %constant.25.clone.refs_5_) | copy-start | bytes 3145732
  27.3 4.9 %copy-start.3 = (bf16[256,2048]{1,0:T(8,128)(2,1)S(1)}, bf16[256,2048]{1,0:T(8,128)(2,1)}, u32[]{:S(2)}) copy-start(bf16[256,2048]{1,0:T(8,128)(2,1)} %constant.24.clone.refs_4_) | copy-start | bytes 3145732
  27.3 4.9 %copy-start.6 = (bf16[512,256]{1,0:T(8,128)(2,1)S(1)}, bf16[512,256]{1,0:T(8,128)(2,1)}, u32[]{:S(2)}) copy-start(bf16[512,256]{1,0:T(8,128)(2,1)} %constant.23.clone.refs_3_) | copy-start | bytes 786436
  27.3 4.9 %copy-start.7 = (bf16[512,256]{1,0:T(8,128)(2,1)S(1)}, bf16[512,256]{1,0:T(8,128)(2,1)}, u32[]{:S(2)}) copy-start(bf16[512,256]{1,0:T(8,128)(2,1)} %constant.22.clone.refs_2_) | copy-start | bytes 786436
  27.3 4.9 %copy-start.10 = (s32[32,1024]{1,0:T(8,128)S(1)}, s32[32,1024]{1,0:T(8,128)}, u32[]{:S(2)}) copy-start(s32[32,1024]{1,0:T(8,128)} %refs_10_.1) | copy-start | bytes 393220
  27.3 4.9 %copy-start.11 = (f32[32,1024]{1,0:T(8,128)S(1)}, f32[32,1024]{1,0:T(8,128)}, u32[]{:S(2)}) copy-start(f32[32,1024]{1,0:T(8,128)} %refs_11_.1) | copy-start | bytes 393220
  27.3 4.9 %copy-start.12 = (s32[32,1024]{1,0:T(8,128)S(1)}, s32[32,1024]{1,0:T(8,128)}, u32[]{:S(2)}) copy-start(s32[32,1024]{1,0:T(8,128)} %refs_12_.1) | copy-start | bytes 393220
  27.3 4.9 %copy-start.13 = (f32[2,16]{1,0:T(2,128)S(1)}, f32[2,16]{1,0:T(2,128)}, u32[]{:S(2)}) copy-start(f32[2,16]{1,0:T(2,128)} %refs_8_.1) | copy-start | bytes 388
  27.3 4.9 %copy-start.14 = (f32[16]{0:T(128)S(1)}, f32[16]{0:T(128)}, u32[]{:S(2)}) copy-start(f32[16]{0:T(128)} %refs_6_.1) | copy-start | bytes 196
  27.3 4.9 %copy-start.15 = (f32[16]{0:T(128)S(1)}, f32[16]{0:T(128)}, u32[]{:S(2)}) copy-start(f32[16]{0:T(128)} %refs_7_.1) | copy-start | bytes 196
  27.4 4.9 %copy-start.16 = (f32[2]{0:T(128)S(1)}, f32[2]{0:T(128)}, u32[]{:S(2)}) copy-start(f32[2]{0:T(128)} %refs_9_.1) | copy-start | bytes 28
  32.3 2.2 %copy-start.1 = (f32[16,32,2048]{2,1,0:T(8,128)S(1)}, f32[16,32,2048]{2,1,0:T(8,128)}, u32[]{:S(2)}) copy-start(f32[16,32,2048]{2,1,0:T(8,128)} %refs_0_.3) | copy-start | bytes 12582916

commit v3 on v2

--- a/solution.py
+++ b/solution.py
@@ -64,17 +64,17 @@
     return one(a[0], b[0]) + (one(a[0], b[1]) + one(a[1], b[0]))
 
 
-def spread(R, me, src, dst, send, recv):
+def spread(R, me, half, src, dst, send, recv):
     chan = lax.axis_index("chan")
     copies = []
     for step in range(1, R):
         to = lax.rem(me + step, R)
         copies.append(
             pltpu.make_async_remote_copy(
-                src_ref=src.at[to],
-                dst_ref=dst.at[me],
-                send_sem=send.at[step],
-                recv_sem=recv.at[step],
+                src_ref=src.at[half, to],
+                dst_ref=dst.at[half, me],
+                send_sem=send.at[half * R + step],
+                recv_sem=recv.at[half * R + step],
                 device_id=(to, chan),
                 device_id_type=MESH,
             )
@@ -92,31 +92,57 @@
     return barrier
 
 
-def forward_kernel(R, hid, fyh, fyl, txh, txl, out, spec, got, xs, chs, chr_, ssem, rsem, csem):
+def forward_kernel(
+    R, hid_in, fyh_in, fyl_in, txh_in, txl_in, out,
+    hid, fyh, fyl, txh, txl, spec, got, xs, chs, chr_, ssem, rsem, csem, lsem,
+):
     me = lax.axis_index("rows")
     chan = lax.axis_index("chan")
     cl, rc, ny = hid.shape
+    ch = cl // 2
+    pairs = [
+        (fyh_in, fyh),
+        (hid_in.at[pl.ds(0, ch)], hid.at[pl.ds(0, ch)]),
+        (fyl_in, fyl),
+        (hid_in.at[pl.ds(ch, ch)], hid.at[pl.ds(ch, ch)]),
+        (txh_in, txh),
+        (txl_in, txl),
+    ]
+    loads = [pltpu.make_async_copy(a, b, lsem.at[n]) for n, (a, b) in enumerate(pairs)]
+    for load in loads:
+        load.start()
     barrier = greet(R, me, chan)
-    acc = jnp.zeros((fyh.shape[0], cl * rc), f32)
     kc = 512
-    for j in range(ny // kc):
-        cols = slice(j * kc, (j + 1) * kc)
-        h = split(hid[:, :, cols].reshape(cl * rc, kc))
-        acc = acc + dot3((fyh[:, cols], fyl[:, cols]), h, NT)
-    spec[...] = acc.reshape(spec.shape)
-    pl.semaphore_wait(barrier, R)
-    copies = spread(R, me, spec, got, ssem, rsem)
-    for copy in copies:
-        copy.start()
-    got[me] = spec[me]
-    for copy in copies:
-        copy.wait()
     half = cl * 8
-    for ri in range(2):
-        for c in range(cl):
-            xs[ri * half + c * 8 : ri * half + c * 8 + 8, :] = jnp.concatenate(
-                [got[s, ri * 8 : ri * 8 + 8, c * rc : (c + 1) * rc] for s in range(R)], axis=1
-            )
+    sent = []
+    for h in range(2):
+        for load in loads[0:3] if h == 0 else loads[3:4]:
+            load.wait()
+        acc = jnp.zeros((fyh.shape[0], ch * rc), f32)
+        for j in range(ny // kc):
+            cols = slice(j * kc, (j + 1) * kc)
+            x = split(hid[h * ch : (h + 1) * ch, :, cols].reshape(ch * rc, kc))
+            acc = acc + dot3((fyh[:, cols], fyl[:, cols]), x, NT)
+        spec[h] = acc.reshape(spec.shape[1:])
+        if h == 0:
+            pl.semaphore_wait(barrier, R)
+        copies = spread(R, me, h, spec, got, ssem, rsem)
+        for copy in copies:
+            copy.start()
+        got[h, me] = spec[h, me]
+        sent.append(copies)
+    for h in range(2):
+        for copy in sent[h]:
+            copy.wait()
+        for ri in range(2):
+            for c in range(ch):
+                at = ri * half + (h * ch + c) * 8
+                xs[at : at + 8, :] = jnp.concatenate(
+                    [got[h, s, ri * 8 : ri * 8 + 8, c * rc : (c + 1) * rc] for s in range(R)],
+                    axis=1,
+                )
+    for load in loads[4:]:
+        load.wait()
     g = dot3((txh[...], txl[...]), split(xs[...]), NT)
     mx = g.shape[0] // 2
     re = g[:mx, :half] + g[mx:, half:]
@@ -140,16 +166,19 @@
 
 
 def inverse_kernel(
-    R, hid, mixd, tih, til, iyh, iyl, gain, bias, pw, pb, mask, front, flags,
+    R, hid_in, mixd, tih, til, iyh, iyl, gain, bias, pw, pb, mask, front, flags,
     vel, nxt,
     mall, chr_, isrc, igot, xs, xth, xtl, spc, psend, pgot, own, phi, ab,
-    ssem, rsem, csem, psem, qsem, hs, hr,
+    ssem, rsem, csem, psem, qsem, hs, hr, hid, lsem,
 ):
     me = lax.axis_index("rows")
     chan = lax.axis_index("chan")
     cl, rc, ny = hid.shape
     half = cl * 8
     tw = ny // 2
+    rh = rc // 2
+    load = pltpu.make_async_copy(hid_in, hid, lsem.at[0])
+    load.start()
     nch = tw // CW
     last = R - 1
     phi[...] = jnp.zeros_like(phi)
@@ -215,69 +244,80 @@
         [jnp.concatenate([re, im], axis=1), jnp.concatenate([-im, re], axis=1)], axis=0
     )
     res = dot3((tih[...], til[...]), split(full), NN)
-    isrc[...] = res.reshape(isrc.shape)
-    copies = spread(R, me, isrc, igot, ssem, rsem)
-    for copy in copies:
-        copy.start()
-    igot[me] = isrc[me]
-    for copy in copies:
-        copy.wait()
-    for s in range(R):
-        t = igot[s].T
-        for ri in range(2):
-            xs[s * 16 + ri * 8 : s * 16 + ri * 8 + 8, :] = jnp.concatenate(
-                [t[ri * half + c * 8 : ri * half + c * 8 + 8, :] for c in range(cl)], axis=1
-            )
-    xt = split(xs[...].T)
-    xth[...] = xt[0]
-    xtl[...] = xt[1]
-
-    def share(col):
+    res = res.reshape(R, 2, rh, 2 * half)
+    sent = []
+    for h in range(2):
+        isrc[h] = res[:, h]
+        copies = spread(R, me, h, isrc, igot, ssem, rsem)
+        for copy in copies:
+            copy.start()
+        igot[h, me] = isrc[h, me]
+        sent.append(copies)
+
+    def share(h, col):
         cols = pl.ds(pl.multiple_of(col, CW), CW)
         spc[...] = dot3((xth[...], xtl[...]), (iyh[:, cols], iyl[:, cols]), NN)
-        u = jnp.zeros((rc, CW), f32)
-        v = jnp.zeros((rc, CW), f32)
+        u = jnp.zeros((rh, CW), f32)
+        v = jnp.zeros((rh, CW), f32)
         for c in range(cl):
-            z = spc[c * rc : (c + 1) * rc, :] + (gain[c] * hid[c, :, cols] + bias[c])
+            skip = gain[c] * hid[c, h * rh : (h + 1) * rh, cols] + bias[c]
+            z = spc[c * rh : (c + 1) * rh, :] + skip
             a = (0.5 * z) * (1.0 + lax.erf(z * (0.5**0.5)))
             u = u + pw[0, c] * a
             v = v + pw[1, c] * a
         return u, v
 
-    def pcopy(j):
+    def pcopy(h, j):
         return pltpu.make_async_remote_copy(
-            src_ref=psend.at[j],
-            dst_ref=pgot.at[j],
-            send_sem=psem.at[j],
-            recv_sem=qsem.at[j],
+            src_ref=psend.at[h, j],
+            dst_ref=pgot.at[h, j],
+            send_sem=psem.at[h * nch + j],
+            recv_sem=qsem.at[h * nch + j],
             device_id=(me, 1 - chan),
             device_id_type=MESH,
         )
 
-    def theirs(j, carry):
-        u, v = share((1 - chan) * tw + j * CW)
-        psend[j, 0] = u
-        psend[j, 1] = v
-        pcopy(j).start()
-        return carry
-
-    def ours(j, carry):
-        u, v = share(chan * tw + j * CW)
-        own[j, 0] = u
-        own[j, 1] = v
-        return carry
-
-    lax.fori_loop(0, nch, theirs, 0)
-    lax.fori_loop(0, nch, ours, 0)
-    for j in range(nch):
-        pcopy(j).wait()
-        cols = slice(j * CW, (j + 1) * CW)
-        ice = mask[:, cols].astype(f32)
-        band = flags[:, cols].astype(f32) * time_step
-        for k in range(2):
-            w = (own[j, k] + pgot[j, k] + pb[k]) * ice
-            vel[k, :, cols] = w
-            ab[k, 8 : 8 + rc, 128 + j * CW : 128 + (j + 1) * CW] = w * band
+    for h in range(2):
+        for copy in sent[h]:
+            copy.wait()
+        for s in range(R):
+            t = igot[h, s].T
+            for ri in range(2):
+                xs[s * 16 + ri * 8 : s * 16 + ri * 8 + 8, :] = jnp.concatenate(
+                    [t[ri * half + c * 8 : ri * half + c * 8 + 8, :] for c in range(cl)], axis=1
+                )
+        xt = split(xs[...].T)
+        xth[...] = xt[0]
+        xtl[...] = xt[1]
+        if h == 0:
+            load.wait()
+
+        def theirs(j, carry):
+            u, v = share(h, (1 - chan) * tw + j * CW)
+            psend[h, j, 0] = u
+            psend[h, j, 1] = v
+            pcopy(h, j).start()
+            return carry
+
+        def ours(j, carry):
+            u, v = share(h, chan * tw + j * CW)
+            own[h, j, 0] = u
+            own[h, j, 1] = v
+            return carry
+
+        lax.fori_loop(0, nch, theirs, 0)
+        lax.fori_loop(0, nch, ours, 0)
+    for h in range(2):
+        rows = slice(h * rh, (h + 1) * rh)
+        for j in range(nch):
+            pcopy(h, j).wait()
+            cols = slice(j * CW, (j + 1) * CW)
+            ice = mask[rows, cols].astype(f32)
+            band = flags[rows, cols].astype(f32) * time_step
+            for k in range(2):
+                w = (own[h, j, k] + pgot[h, j, k] + pb[k]) * ice
+                vel[k, rows, cols] = w
+                ab[k, 8 + h * rh : 8 + (h + 1) * rh, 128 + j * CW : 128 + (j + 1) * CW] = w * band
     halo(1, ab, "start")
     halo(0, phi, "wait")
     halo(1, ab, "wait")
@@ -314,6 +354,8 @@
     tx = np.concatenate([np.cos(xph), np.sin(xph)], axis=0)
     vm = pl.BlockSpec(memory_space=pltpu.VMEM)
     sm = pl.BlockSpec(memory_space=pltpu.SMEM)
+    hbm = pl.BlockSpec(memory_space=pltpu.HBM)
+    bf16 = jnp.bfloat16
     dma = pltpu.SemaphoreType.DMA
     lanes = cl * ql
 
@@ -326,17 +368,23 @@
     spec = pl.pallas_call(
         kernel_a,
         out_shape=jax.ShapeDtypeStruct((D, 2, pn, lanes), f32),
-        in_specs=[vm] * 5,
+        in_specs=[hbm] * 5,
         out_specs=vm,
         scratch_shapes=[
-            pltpu.VMEM((R, 2 * ql, cl * rc), f32),
-            pltpu.VMEM((R, 2 * ql, cl * rc), f32),
+            pltpu.VMEM((cl, rc, ny), f32),
+            pltpu.VMEM((2 * my, ny), bf16),
+            pltpu.VMEM((2 * my, ny), bf16),
+            pltpu.VMEM((2 * mx, nx), bf16),
+            pltpu.VMEM((2 * mx, nx), bf16),
+            pltpu.VMEM((2, R, 2 * ql, cl // 2 * rc), f32),
+            pltpu.VMEM((2, R, 2 * ql, cl // 2 * rc), f32),
             pltpu.VMEM((2 * lanes, nx), f32),
             pltpu.VMEM((D, 2, pn, lanes), f32),
             pltpu.VMEM((2, pn, lanes), f32),
-            dma((R,)),
-            dma((R,)),
+            dma((2 * R,)),
+            dma((2 * R,)),
             dma((2,)),
+            dma((6,)),
         ],
         compiler_params=pltpu.CompilerParams(
             collective_id=0, has_side_effects=True, vmem_limit_bytes=40 * 2**20
@@ -358,29 +406,31 @@
             jax.ShapeDtypeStruct((2, rc, tw), f32),
             jax.ShapeDtypeStruct((rc, tw), f32),
         ),
-        in_specs=[vm] * 6 + [sm] * 4 + [vm] * 3,
+        in_specs=[hbm] + [vm] * 5 + [sm] * 4 + [vm] * 3,
         out_specs=(vm, vm),
         scratch_shapes=[
             pltpu.VMEM((D, 2, pn, lanes), f32),
             pltpu.VMEM((2, pn, lanes), f32),
-            pltpu.VMEM((R, rc, 2 * lanes), f32),
-            pltpu.VMEM((R, rc, 2 * lanes), f32),
-            pltpu.VMEM((2 * my, cl * rc), f32),
-            pltpu.VMEM((cl * rc, 2 * my), jnp.bfloat16),
-            pltpu.VMEM((cl * rc, 2 * my), jnp.bfloat16),
-            pltpu.VMEM((cl * rc, CW), f32),
-            pltpu.VMEM((nch, 2, rc, CW), f32),
-            pltpu.VMEM((nch, 2, rc, CW), f32),
-            pltpu.VMEM((nch, 2, rc, CW), f32),
+            pltpu.VMEM((2, R, rc // 2, 2 * lanes), f32),
+            pltpu.VMEM((2, R, rc // 2, 2 * lanes), f32),
+            pltpu.VMEM((2 * my, cl * rc // 2), f32),
+            pltpu.VMEM((cl * rc // 2, 2 * my), bf16),
+            pltpu.VMEM((cl * rc // 2, 2 * my), bf16),
+            pltpu.VMEM((cl * rc // 2, CW), f32),
+            pltpu.VMEM((2, nch, 2, rc // 2, CW), f32),
+            pltpu.VMEM((2, nch, 2, rc // 2, CW), f32),
+            pltpu.VMEM((2, nch, 2, rc // 2, CW), f32),
             pltpu.VMEM((rc + 16, tw + 256), f32),
             pltpu.VMEM((2, rc + 16, tw + 256), f32),
-            dma((R,)),
-            dma((R,)),
+            dma((2 * R,)),
+            dma((2 * R,)),
             dma((2,)),
-            dma((nch,)),
-            dma((nch,)),
+            dma((2 * nch,)),
+            dma((2 * nch,)),
             dma((10,)),
             dma((10,)),
+            pltpu.VMEM((cl, rc, ny), f32),
+            dma((1,)),
         ],
         compiler_params=pltpu.CompilerParams(
             collective_id=1, has_side_effects=True, vmem_limit_bytes=40 * 2**20
@@ -407,7 +457,7 @@
     R = lax.axis_size("rows")
     D = lax.axis_size("chan")
     ql = spectral_weight.shape[1]
-    if D == 2 and ql == 8 and cl * ql == 128 and rc % 8 == 0 and (rc * R) % 128 == 0:
+    if D == 2 and ql == 8 and cl * ql == 128 and rc % 16 == 0 and (rc * R) % 128 == 0:
         return on_kernels(
             hidden, front, spectral_weight, skip_gain, skip_bias, project_weight,
             project_bias, ice_mask, front_flags,

time: 71.9 us -> 72.6 us (level)
  Pallas kernels: 54.7 us -> 55.6 us
    pallas_call x1, Pallas kernels: 19.8 us -> 21.5 us  [on_kernels(): pl.pallas_call(kernel_a, out_shape=jax.ShapeDtypeStruct((D, 2, pn, lanes)...]
    pallas_call x1, Pallas kernels: 34.9 us -> 34.1 us  [on_kernels(): pl.pallas_call(kernel_b, out_shape=(jax.ShapeDtypeStruct((2, rc, tw), f32...]
where the time goes in v3:
time: 72.6 us; the launch traced here: 71.6 us
  Pallas kernels  55.6 us (77%)
  local copies, waits for them, and re-layouts  10.6 us (15%)
  other arithmetic  4.48 us (6%)
  between operations  0.91 us (1%)
    pallas_call x1, Pallas kernels, on_kernels(): pl.pallas_call(kernel_b, out_shape=(jax.ShapeDtypeStruct((2, rc, tw), f32...  34.1 us
    pallas_call x1, Pallas kernels, on_kernels(): pl.pallas_call(kernel_a, out_shape=jax.ShapeDtypeStruct((D, 2, pn, lanes)...  21.5 us
    unnamed x36, local copies, waits for them, and re-layouts  10.1 us
    reduce_sum x1, other arithmetic, on_kernels(): re = jnp.sum(wt[0] * a - wt[1] * b, axis=0)  4.45 us

profile of v3, /device:TPU:3, one launch (start us, length us, event | category | flops | bytes accessed | tf_op | source)
XLA Modules:
  0.0 71.6 jit_solution(8068300803906377241)
XLA Ops:
  0.6 0.0 copy-start
  0.6 2.2 %copy-done = f32[16,32,2048]{2,1,0:T(8,128)S(1)} copy-done((f32[16,32,2048]{2,1,0:T(8,128)S(1)}, f32[16,32,2048]{2,1,0:T(8,128)}, u32[]{:S(2)}) %copy-start) | copy-done | bytes 4194328
  2.8 0.0 copy-start.4
  2.8 1.2 %copy-done.4 = bf16[256,2048]{1,0:T(8,128)(2,1)S(1)} copy-done((bf16[256,2048]{1,0:T(8,128)(2,1)S(1)}, bf16[256,2048]{1,0:T(8,128)(2,1)}, u32[]{:S(2)}) %copy-start.4) | copy-done | bytes 1048600
  4.0 0.0 copy-start.5
  4.0 1.2 %copy-done.5 = bf16[256,2048]{1,0:T(8,128)(2,1)S(1)} copy-done((bf16[256,2048]{1,0:T(8,128)(2,1)S(1)}, bf16[256,2048]{1,0:T(8,128)(2,1)}, u32[]{:S(2)}) %copy-start.5) | copy-done | bytes 1048600
  5.3 0.0 copy-start.8
  5.3 0.9 %copy-done.8 = bf16[256,512]{1,0:T(8,128)(2,1)S(1)} copy-done((bf16[256,512]{1,0:T(8,128)(2,1)S(1)}, bf16[256,512]{1,0:T(8,128)(2,1)}, u32[]{:S(2)}) %copy-start.8) | copy-done | bytes 262168
  6.2 0.0 copy-start.9
  6.2 0.9 %copy-done.9 = bf16[256,512]{1,0:T(8,128)(2,1)S(1)} copy-done((bf16[256,512]{1,0:T(8,128)(2,1)S(1)}, bf16[256,512]{1,0:T(8,128)(2,1)}, u32[]{:S(2)}) %copy-start.9) | copy-done | bytes 262168
  7.2 21.5 %forward.1 = f32[2,2,64,128]{3,2,1,0:T(8,128)S(1)} custom-call(f32[16,32,2048]{2,1,0:T(8,128)S(1)} %copy-done, bf16[256,2048]{1,0:T(8,128)(2,1)S(1)} %copy-done.5, bf16[256,2048]{1,0:T(8,128)(2,1)S(1)} %copy-done.4, bf16[256,512]{1,0:T(8,128)(2,1)S(1)} %copy-done.9, bf16[256,512]{1,0:T(8,128)(2,1)S(1)} %copy-done.8), custom_call_target="tpu_custom_call" | custom-call | tf_op jit(solution)/shard_map/forward/pallas_call | solution.py:368
  28.7 0.1 copy.24
  28.9 0.0 copy-start.2
  29.0 0.0 copy-start.3
  29.0 0.0 copy-start.6
  29.0 0.0 copy-start.7
  29.0 0.0 copy-start.10
  29.0 0.0 copy-start.11
  29.0 0.0 copy-start.12
  29.0 0.0 copy-start.13
  29.0 0.0 copy-start.14
  29.1 0.0 copy-start.15
  29.1 0.0 copy-start.16
  29.1 4.5 %subtract_reduce_fusion = (f32[32,8,64]{2,0,1:T(8,128)S(1)}, f32[32,8,64]{2,0,1:T(8,128)S(1)}) fusion(f32[2,32,32,8,64]{4,2,1,3,0:T(8,128)} %bitcast.24, f32[32,8,64]{2,0,1:T(8,128)S(1)} %copy.26, f32[32,8,64]{2,0,1:T(8,128)S(1)} %copy.25), kind=kLoop, calls=%fused_computation.3 | loop fusion | flops 4161536 | bytes 4456448 | tf_op jit(solution)/shard_map/reduce_sum | solution.py:397
  33.5 0.1 copy.27
  33.6 0.1 copy.28
  33.7 0.1 copy.30.refs_1_
  33.9 0.0 copy-done.2
  33.9 0.0 copy-done.3
  33.9 0.0 copy-done.6
  33.9 0.0 copy-done.7
  33.9 0.0 copy-done.10
  33.9 0.0 copy-done.11
  33.9 0.0 copy-done.12
  33.9 0.0 copy-done.13
  33.9 0.0 copy-done.14
  34.0 0.0 copy-done.15
  34.0 0.0 copy-done.16
  34.0 0.0 copy-start.1
  34.0 2.2 %copy-done.1 = f32[16,32,2048]{2,1,0:T(8,128)S(1)} copy-done((f32[16,32,2048]{2,1,0:T(8,128)S(1)}, f32[16,32,2048]{2,1,0:T(8,128)}, u32[]{:S(2)}) %copy-start.1) | copy-done | bytes 4194328
  36.2 34.1 %inverse.1 = (f32[2,32,1024]{2,1,0:T(8,128)S(1)}, f32[32,1024]{1,0:T(8,128)S(1)}) custom-call(f32[16,32,2048]{2,1,0:T(8,128)S(1)} %copy-done.1, f32[2,2,64,128]{3,2,1,0:T(8,128)S(1)} %copy.30.refs_1_, bf16[512,256]{1,0:T(8,128)(2,1)S(1)} %copy-done.7, bf16[512,256]{1,0:T(8,128)(2,1)S(1)} %copy-done.6, bf16[256,2048]{1,0:T(8,128)(2,1)S(1)} %copy-done.3, ...), custom_call_target="tpu_custom_call" | custom-call | tf_op jit(solution)/shard_map/inverse/pallas_call | solution.py:403
  70.3 0.7 copy.35
  71.0 0.7 copy.36
  (4 shorter events, 0.1 us)
Async XLA Ops:
  0.6 2.2 %copy-start = (f32[16,32,2048]{2,1,0:T(8,128)S(1)}, f32[16,32,2048]{2,1,0:T(8,128)}, u32[]{:S(2)}) copy-start(f32[16,32,2048]{2,1,0:T(8,128)} %refs_0_.3) | copy-start | bytes 12582916
  2.8 1.2 %copy-start.4 = (bf16[256,2048]{1,0:T(8,128)(2,1)S(1)}, bf16[256,2048]{1,0:T(8,128)(2,1)}, u32[]{:S(2)}) copy-start(bf16[256,2048]{1,0:T(8,128)(2,1)} %constant.19.clone.refs_2_) | copy-start | bytes 3145732
  4.0 1.2 %copy-start.5 = (bf16[256,2048]{1,0:T(8,128)(2,1)S(1)}, bf16[256,2048]{1,0:T(8,128)(2,1)}, u32[]{:S(2)}) copy-start(bf16[256,2048]{1,0:T(8,128)(2,1)} %constant.18.clone.refs_1_) | copy-start | bytes 3145732
  5.3 0.9 %copy-start.8 = (bf16[256,512]{1,0:T(8,128)(2,1)S(1)}, bf16[256,512]{1,0:T(8,128)(2,1)}, u32[]{:S(2)}) copy-start(bf16[256,512]{1,0:T(8,128)(2,1)} %constant.21.clone.refs_4_) | copy-start | bytes 786436
  6.2 0.9 %copy-start.9 = (bf16[256,512]{1,0:T(8,128)(2,1)S(1)}, bf16[256,512]{1,0:T(8,128)(2,1)}, u32[]{:S(2)}) copy-start(bf16[256,512]{1,0:T(8,128)(2,1)} %constant.20.clone.refs_3_) | copy-start | bytes 786436
  28.9 4.9 %copy-start.2 = (bf16[256,2048]{1,0:T(8,128)(2,1)S(1)}, bf16[256,2048]{1,0:T(8,128)(2,1)}, u32[]{:S(2)}) copy-start(bf16[256,2048]{1,0:T(8,128)(2,1)} %constant.25.clone.refs_5_) | copy-start | bytes 3145732
  29.0 4.9 %copy-start.3 = (bf16[256,2048]{1,0:T(8,128)(2,1)S(1)}, bf16[256,2048]{1,0:T(8,128)(2,1)}, u32[]{:S(2)}) copy-start(bf16[256,2048]{1,0:T(8,128)(2,1)} %constant.24.clone.refs_4_) | copy-start | bytes 3145732
  29.0 4.9 %copy-start.6 = (bf16[512,256]{1,0:T(8,128)(2,1)S(1)}, bf16[512,256]{1,0:T(8,128)(2,1)}, u32[]{:S(2)}) copy-start(bf16[512,256]{1,0:T(8,128)(2,1)} %constant.23.clone.refs_3_) | copy-start | bytes 786436
  29.0 4.9 %copy-start.7 = (bf16[512,256]{1,0:T(8,128)(2,1)S(1)}, bf16[512,256]{1,0:T(8,128)(2,1)}, u32[]{:S(2)}) copy-start(bf16[512,256]{1,0:T(8,128)(2,1)} %constant.22.clone.refs_2_) | copy-start | bytes 786436
  29.0 4.9 %copy-start.10 = (s32[32,1024]{1,0:T(8,128)S(1)}, s32[32,1024]{1,0:T(8,128)}, u32[]{:S(2)}) copy-start(s32[32,1024]{1,0:T(8,128)} %refs_10_.1) | copy-start | bytes 393220
  29.0 4.9 %copy-start.11 = (f32[32,1024]{1,0:T(8,128)S(1)}, f32[32,1024]{1,0:T(8,128)}, u32[]{:S(2)}) copy-start(f32[32,1024]{1,0:T(8,128)} %refs_11_.1) | copy-start | bytes 393220
  29.0 4.9 %copy-start.12 = (s32[32,1024]{1,0:T(8,128)S(1)}, s32[32,1024]{1,0:T(8,128)}, u32[]{:S(2)}) copy-start(s32[32,1024]{1,0:T(8,128)} %refs_12_.1) | copy-start | bytes 393220
  29.0 4.9 %copy-start.13 = (f32[2,16]{1,0:T(2,128)S(1)}, f32[2,16]{1,0:T(2,128)}, u32[]{:S(2)}) copy-start(f32[2,16]{1,0:T(2,128)} %refs_8_.1) | copy-start | bytes 388
  29.0 4.9 %copy-start.14 = (f32[16]{0:T(128)S(1)}, f32[16]{0:T(128)}, u32[]{:S(2)}) copy-start(f32[16]{0:T(128)} %refs_6_.1) | copy-start | bytes 196
  29.1 4.9 %copy-start.15 = (f32[16]{0:T(128)S(1)}, f32[16]{0:T(128)}, u32[]{:S(2)}) copy-start(f32[16]{0:T(128)} %refs_7_.1) | copy-start | bytes 196
  29.1 4.9 %copy-start.16 = (f32[2]{0:T(128)S(1)}, f32[2]{0:T(128)}, u32[]{:S(2)}) copy-start(f32[2]{0:T(128)} %refs_9_.1) | copy-start | bytes 28
  34.0 2.2 %copy-start.1 = (f32[16,32,2048]{2,1,0:T(8,128)S(1)}, f32[16,32,2048]{2,1,0:T(8,128)}, u32[]{:S(2)}) copy-start(f32[16,32,2048]{2,1,0:T(8,128)} %refs_0_.3) | copy-start | bytes 12582916

commit v4 on v3

--- a/solution.py
+++ b/solution.py
@@ -166,10 +166,11 @@
 
 
 def inverse_kernel(
-    R, hid_in, mixd, tih, til, iyh, iyl, gain, bias, pw, pb, mask, front, flags,
+    R, hid_in, mixd, tih_in, til_in, iyh_in, iyl_in, gain, bias, pw, pb, mask_in, front, flags_in,
     vel, nxt,
     mall, chr_, isrc, igot, xs, xth, xtl, spc, psend, pgot, own, phi, ab,
-    ssem, rsem, csem, psem, qsem, hs, hr, hid, lsem,
+    ssem, rsem, csem, psem, qsem, hs, hr,
+    hid, tih, til, iyh, iyl, mask, flags, lsem,
 ):
     me = lax.axis_index("rows")
     chan = lax.axis_index("chan")
@@ -177,8 +178,13 @@
     half = cl * 8
     tw = ny // 2
     rh = rc // 2
-    load = pltpu.make_async_copy(hid_in, hid, lsem.at[0])
-    load.start()
+    pairs = [
+        (tih_in, tih), (til_in, til), (hid_in, hid), (iyh_in, iyh), (iyl_in, iyl),
+        (mask_in, mask), (flags_in, flags),
+    ]
+    loads = [pltpu.make_async_copy(a, b, lsem.at[n]) for n, (a, b) in enumerate(pairs)]
+    for load in loads:
+        load.start()
     nch = tw // CW
     last = R - 1
     phi[...] = jnp.zeros_like(phi)
@@ -243,6 +249,8 @@
     full = jnp.concatenate(
         [jnp.concatenate([re, im], axis=1), jnp.concatenate([-im, re], axis=1)], axis=0
     )
+    for load in loads[:2]:
+        load.wait()
     res = dot3((tih[...], til[...]), split(full), NN)
     res = res.reshape(R, 2, rh, 2 * half)
     sent = []
@@ -290,7 +298,8 @@
         xth[...] = xt[0]
         xtl[...] = xt[1]
         if h == 0:
-            load.wait()
+            for load in loads[2:]:
+                load.wait()
 
         def theirs(j, carry):
             u, v = share(h, (1 - chan) * tw + j * CW)
@@ -387,7 +396,7 @@
             dma((6,)),
         ],
         compiler_params=pltpu.CompilerParams(
-            collective_id=0, has_side_effects=True, vmem_limit_bytes=40 * 2**20
+            collective_id=0, has_side_effects=True, vmem_limit_bytes=60 * 2**20
         ),
         name="forward",
     )(hidden, *np_split(fy), *np_split(tx))
@@ -406,7 +415,7 @@
             jax.ShapeDtypeStruct((2, rc, tw), f32),
             jax.ShapeDtypeStruct((rc, tw), f32),
         ),
-        in_specs=[hbm] + [vm] * 5 + [sm] * 4 + [vm] * 3,
+        in_specs=[hbm, vm] + [hbm] * 4 + [sm] * 4 + [hbm, vm, hbm],
         out_specs=(vm, vm),
         scratch_shapes=[
             pltpu.VMEM((D, 2, pn, lanes), f32),
@@ -430,10 +439,16 @@
             dma((10,)),
             dma((10,)),
             pltpu.VMEM((cl, rc, ny), f32),
-            dma((1,)),
+            pltpu.VMEM((nx, 2 * mx), bf16),
+            pltpu.VMEM((nx, 2 * mx), bf16),
+            pltpu.VMEM((2 * my, ny), bf16),
+            pltpu.VMEM((2 * my, ny), bf16),
+            pltpu.VMEM((rc, tw), jnp.int32),
+            pltpu.VMEM((rc, tw), jnp.int32),
+            dma((7,)),
         ],
         compiler_params=pltpu.CompilerParams(
-            collective_id=1, has_side_effects=True, vmem_limit_bytes=40 * 2**20
+            collective_id=1, has_side_effects=True, vmem_limit_bytes=57 * 2**20
         ),
         name="inverse",
     )(

time: 72.6 us -> 67.8 us (0.934)
  local copies, waits for them, and re-layouts: 10.6 us -> 5.28 us
  Pallas kernels: 55.6 us -> 56.7 us
    unnamed x36 -> x2, local copies, waits for them, and re-layouts: 10.1 us -> 3.24 us
    pallas_call x1, Pallas kernels: 21.5 us -> 23.2 us  [on_kernels(): pl.pallas_call(kernel_a, out_shape=jax.ShapeDtypeStruct((D, 2, pn, lanes)...]
    pallas_call x1, local copies, waits for them, and re-layouts: 0.13 us -> 1.03 us  [on_kernels(): pl.pallas_call(kernel_a, out_shape=jax.ShapeDtypeStruct((D, 2, pn, lanes)...]
where the time goes in v4:
time: 67.8 us; the launch traced here: 67.1 us
  Pallas kernels  56.7 us (84%)
  local copies, waits for them, and re-layouts  5.28 us (8%)
  other arithmetic  4.34 us (6%)
  between operations  0.7 us (1%)
    pallas_call x1, Pallas kernels, on_kernels(): pl.pallas_call(kernel_b, out_shape=(jax.ShapeDtypeStruct((2, rc, tw), f32...  33.5 us
    pallas_call x1, Pallas kernels, on_kernels(): pl.pallas_call(kernel_a, out_shape=jax.ShapeDtypeStruct((D, 2, pn, lanes)...  23.2 us
    reduce_sum x1, other arithmetic, on_kernels(): re = jnp.sum(wt[0] * a - wt[1] * b, axis=0)  4.32 us
    unnamed x2, local copies, waits for them, and re-layouts  3.24 us

profile of v4, /device:TPU:3, one launch (start us, length us, event | category | flops | bytes accessed | tf_op | source)
XLA Modules:
  0.0 67.1 jit_solution(12471564299990959596)
XLA Ops:
  0.6 23.2 %forward.1 = f32[2,2,64,128]{3,2,1,0:T(8,128)} custom-call(f32[16,32,2048]{2,1,0:T(8,128)} %refs_0_.3, bf16[256,2048]{1,0:T(8,128)(2,1)} %constant.18.clone.refs_1_, bf16[256,2048]{1,0:T(8,128)(2,1)} %constant.19.clone.refs_2_, bf16[256,512]{1,0:T(8,128)(2,1)} %constant.20.clone.refs_3_, bf16[256,512]{1,0:T(8,128)(2,1)} %constant.21.clone.refs_4_), custom_call_target="tpu_custom_call" | custom-call | tf_op jit(solution)/shard_map/forward/pallas_call | solution.py:377
  23.9 1.0 %copy.24 = f32[2,2,64,128]{2,3,1,0:T(8,128)S(1)} copy(f32[2,2,64,128]{3,2,1,0:T(8,128)} %forward.1) | data formatting | bytes 262144 | tf_op jit(solution)/shard_map/forward/pallas_call | solution.py:377
  25.0 4.3 %subtract_reduce_fusion = (f32[32,8,64]{2,0,1:T(8,128)S(1)}, f32[32,8,64]{2,0,1:T(8,128)S(1)}) fusion(f32[2,32,32,8,64]{4,2,1,3,0:T(8,128)} %bitcast.24, f32[32,8,64]{2,0,1:T(8,128)S(1)} %copy.26, f32[32,8,64]{2,0,1:T(8,128)S(1)} %copy.25), kind=kLoop, calls=%fused_computation.3 | loop fusion | flops 4161536 | bytes 4456448 | tf_op jit(solution)/shard_map/reduce_sum | solution.py:406
  29.3 0.1 copy.27
  29.4 0.1 copy.28
  29.5 0.8 %copy.30.refs_1_ = f32[2,2,64,128]{3,2,1,0:T(8,128)} copy(f32[2,2,64,128]{2,3,0,1:T(8,128)S(1)} %maximum_bitcast_fusion) | data formatting | bytes 262144 | tf_op jit(solution)/shard_map/reshape | solution.py:409
  30.3 33.5 %inverse.1 = (f32[2,32,1024]{2,1,0:T(8,128)}, f32[32,1024]{1,0:T(8,128)}) custom-call(f32[16,32,2048]{2,1,0:T(8,128)} %refs_0_.3, f32[2,2,64,128]{3,2,1,0:T(8,128)} %copy.30.refs_1_, bf16[512,256]{1,0:T(8,128)(2,1)} %constant.22.clone.refs_2_, bf16[512,256]{1,0:T(8,128)(2,1)} %constant.23.clone.refs_3_, bf16[256,2048]{1,0:T(8,128)(2,1)} %constant.24.clone.refs_4_, ...), custom_call_target="tpu_custom_call" | custom-call | tf_op jit(solution)/shard_map/inverse/pallas_call | solution.py:412
  63.8 1.7 %copy.35 = f32[2,32,1024]{2,1,0:T(8,128)} copy(f32[2,32,1024]{2,1,0:T(8,128)} %get-tuple-element.8) | data formatting | bytes 524288
  65.5 1.6 %copy.36 = f32[32,1024]{1,0:T(8,128)} copy(f32[32,1024]{1,0:T(8,128)} %get-tuple-element.9) | data formatting | bytes 262144
  (4 shorter events, 0.1 us)
